TPU v7x, 32 devices: a whole 2x2x4 slice. The times are simulated.
32 devices in a mesh: ctx: 8 (over z, y), exp: 2 (over x), dp: 2 (over core).
Axes of the slice: x: 2, y: 2, z: 4, core: 2. Of those that a mesh axis runs over, the one named last changes fastest.
Arguments:
- hidden_in: bfloat16 [2, 2048, 1024], P('dp', ('ctx', 'exp')), may hold values from -6 to 6
- queries: bfloat16 [2, 2048, 1024], P('dp', ('ctx', 'exp')), may hold values from -6 to 6
- keys: bfloat16 [2, 2048, 1024], P('dp', ('ctx', 'exp')), may hold values from -6 to 6
- values: bfloat16 [2, 2048, 1024], P('dp', ('ctx', 'exp')), may hold values from -6 to 6
- log_decay: float32 [2, 2048, 8], P('dp', ('ctx', 'exp')), may hold values from -1 to 0
- retention_gain: float32 [1024], replicated, may hold values from 0.25 to 1.75
- norm_gain: float32 [1024], replicated, may hold values from 0.25 to 1.75
- routes: int32 [2, 2048, 2], P('dp', ('ctx', 'exp')), may hold values from 0 to 15, all different within a row; in each aligned block of 128 rows (0 to 127, 128 to 255, ..., all dimensions but the last counted through in order) at most 20 rows name the same one
- route_weights: float32 [2, 2048, 2], P('dp', ('ctx', 'exp')), may hold values from 0.1 to 1
- w_gate: bfloat16 [16, 1024, 1408], P(('ctx', 'dp'), 'exp'), may hold values from -0.1875 to 0.1875
- w_up: bfloat16 [16, 1024, 1408], P(('ctx', 'dp'), 'exp'), may hold values from -0.1875 to 0.1875
- w_down: bfloat16 [16, 1024, 1408], P(('ctx', 'dp'), 'exp'), may hold values from -0.15625 to 0.15625
Outputs:
- output: bfloat16 [2, 2048, 1024], P('dp', ('ctx', 'exp'))
Inputs may be any that keep to these rules, and one draw needn't show every extreme that they name: `routes`: in each aligned block of 128 positions (the positions of one device) no expert is named more than 20 times, and a position's 2 experts differ.
All inputs are finite; a program needn't handle non-finite values.
Results may differ from a plain program's by a relative error of at most 0.007.
Values may be sent and summed in bfloat16 or wider, within the bound.
A program may use at most 128 MiB of HBM per device.

v0:
```python
import jax
import jax.numpy as jnp
from jax import lax
from jax.sharding import PartitionSpec as P


def carried_in(part, axis, combine, identity):
    place = lax.axis_index(axis)
    gathered = jax.tree.map(lambda a: lax.all_gather(a, axis), part)
    state = jax.tree.map(lambda a, e: jnp.zeros_like(a) + jnp.asarray(e, a.dtype), part, identity)

    def one(lap, state):
        return combine(
            state, jax.tree.map(lambda a: lax.dynamic_index_in_dim(a, lap, 0, False), gathered)
        )

    return lax.fori_loop(0, place, one, state)


def rotate(vectors, token_position):
    half_dim = vectors.shape[-1] // 2
    inverse = 10000.0 ** (-jnp.arange(half_dim, dtype=jnp.float32) / half_dim)
    angles = token_position.astype(jnp.float32)[:, None] * inverse[None, :]
    cosine = jnp.cos(angles)[:, None, :]
    sine_part = jnp.sin(angles)[:, None, :]
    leading = vectors[..., :half_dim]
    trailing = vectors[..., half_dim:]
    return jnp.concatenate(
        [leading * cosine - trailing * sine_part, trailing * cosine + leading * sine_part], axis=-1
    )


def chain_combine(earlier, later_part):
    return (earlier[0] * later_part[0], later_part[0][:, None, None] * earlier[1] + later_part[1])


def body(
    hidden_in,
    queries,
    keys,
    values,
    log_decay,
    retention_gain,
    norm_gain,
    routes,
    route_weights,
    w_gate,
    w_up,
    w_down,
):
    tok_rows = hidden_in.shape[1]
    model_width = hidden_in.shape[2]
    head_count = log_decay.shape[2]
    head_dim = model_width // head_count
    block_index = lax.axis_index("ctx") * lax.axis_size("exp") + lax.axis_index("exp")
    token_position = block_index * tok_rows + jnp.arange(tok_rows, dtype=jnp.int32)
    per_head_queries = (
        rotate(
            queries[0].astype(jnp.float32).reshape(tok_rows, head_count, head_dim), token_position
        )
        * head_dim ** (-0.5)
    ).astype(jnp.bfloat16)
    per_head_keys = rotate(
        keys[0].astype(jnp.float32).reshape(tok_rows, head_count, head_dim), token_position
    ).astype(jnp.bfloat16)
    per_head_values = values[0].reshape(tok_rows, head_count, head_dim)
    running_total = jnp.cumsum(log_decay[0], axis=0)
    scores = jnp.einsum(
        "thd,shd->hts", per_head_queries, per_head_keys, preferred_element_type=jnp.float32
    )
    causal = jnp.arange(tok_rows)[:, None] >= jnp.arange(tok_rows)[None, :]
    spread = running_total.T[:, :, None] - running_total.T[:, None, :]
    weights = jnp.where(
        causal[None], scores * jnp.exp(jnp.where(causal[None], spread, 0.0)), 0.0
    ).astype(jnp.bfloat16)
    inside = jnp.einsum(
        "hts,shd->thd", weights, per_head_values, preferred_element_type=jnp.float32
    )
    trailing_decay = jnp.exp(running_total[-1][None, :] - running_total)
    block_summary = jnp.einsum(
        "qpf,qpy->pfy",
        per_head_keys.astype(jnp.float32) * trailing_decay[:, :, None],
        per_head_values.astype(jnp.float32),
        precision=lax.Precision.HIGHEST,
    )
    group_logs, group_sums = (
        lax.all_gather(running_total[-1][None], "exp", axis=0, tiled=True),
        lax.all_gather(block_summary[None], "exp", axis=0, tiled=True),
    )
    group_size = lax.axis_size("exp")
    own_member = lax.axis_index("exp")
    inclusive = jnp.cumsum(group_logs, axis=0)
    exclusive = inclusive - group_logs
    entering_log = lax.dynamic_index_in_dim(exclusive, own_member, 0, keepdims=False)
    before_me = jnp.arange(group_size, dtype=jnp.int32)[:, None] < own_member
    inner_coeff = jnp.where(
        before_me, jnp.exp(jnp.where(before_me, entering_log[None, :] - inclusive, 0.0)), 0.0
    )
    inner_state = jnp.einsum(
        "jh,jhab->hab", inner_coeff, group_sums, precision=lax.Precision.HIGHEST
    )
    total_coeff = jnp.exp(inclusive[-1][None, :] - inclusive)
    group_state = jnp.einsum(
        "jh,jhab->hab", total_coeff, group_sums, precision=lax.Precision.HIGHEST
    )
    group_decay = jnp.exp(inclusive[-1])
    identity = (
        jnp.ones((head_count,), jnp.float32),
        jnp.zeros((head_count, head_dim, head_dim), jnp.float32),
    )
    leading_sum = carried_in((group_decay, group_state), "ctx", chain_combine, identity)
    state_in = jnp.exp(entering_log)[:, None, None] * leading_sum[1] + inner_state
    external_part = jnp.exp(running_total)[:, :, None] * jnp.einsum(
        "wjc,jco->wjo",
        per_head_queries.astype(jnp.float32),
        state_in,
        precision=lax.Precision.HIGHEST,
    )
    retrieved = inside + external_part
    centre = jnp.mean(retrieved, axis=-1, keepdims=True)
    deviation = retrieved - centre
    variance = jnp.mean(deviation * deviation, axis=-1, keepdims=True)
    normalized = (deviation * lax.rsqrt(variance + 1e-05)).reshape(tok_rows, model_width)
    residual = hidden_in[0].astype(jnp.float32) + retention_gain * normalized
    square_mean = jnp.mean(residual * residual, axis=-1, keepdims=True)
    normed = (residual * lax.rsqrt(square_mean + 1e-06) * norm_gain).astype(jnp.bfloat16)
    expert_count = lax.axis_size("ctx") * lax.axis_size("dp")
    top_count = routes.shape[2]
    capacity = (tok_rows * top_count * 5 + 4 * expert_count - 1) // (4 * expert_count)
    slot_count = expert_count * capacity
    route_rows = routes[0]
    expert_hits = (
        route_rows.reshape(tok_rows * top_count)[:, None]
        == jnp.arange(expert_count, dtype=jnp.int32)[None, :]
    ).astype(jnp.int32)
    earlier = jnp.cumsum(expert_hits, axis=0) - expert_hits
    slot_rank = jnp.sum(earlier * expert_hits, axis=1).reshape(tok_rows, top_count)
    destination = route_rows * capacity + slot_rank
    slot_lanes = jnp.arange(slot_count, dtype=jnp.int32)
    placing = jnp.any(destination[None, :, :] == slot_lanes[:, None, None], axis=2).astype(
        jnp.bfloat16
    )
    outgoing = jnp.dot(placing, normed, preferred_element_type=jnp.float32).astype(jnp.bfloat16)
    arrived = lax.all_to_all(
        outgoing.reshape(expert_count, capacity, model_width),
        ("ctx", "dp"),
        split_axis=0,
        concat_axis=0,
        tiled=True,
    ).reshape(slot_count, model_width)
    gate_next = jnp.dot(
        arrived,
        lax.all_gather(w_gate, "exp", axis=1, tiled=True)[0],
        preferred_element_type=jnp.float32,
    )
    up_next = jnp.dot(
        arrived,
        lax.all_gather(w_up, "exp", axis=1, tiled=True)[0],
        preferred_element_type=jnp.float32,
    )
    hidden = (jax.nn.silu(gate_next) * up_next).astype(jnp.bfloat16)
    expert_out = lax.dot_general(
        hidden,
        lax.all_gather(w_down, "exp", axis=1, tiled=True)[0],
        (((1,), (1,)), ((), ())),
        preferred_element_type=jnp.float32,
    ).astype(jnp.bfloat16)
    returned = lax.all_to_all(
        expert_out.reshape(expert_count, capacity, model_width),
        ("ctx", "dp"),
        split_axis=0,
        concat_axis=0,
        tiled=True,
    ).reshape(slot_count, model_width)
    output = residual
    for route_index in range(top_count):
        picking = (destination[:, route_index][:, None] == slot_lanes[None, :]).astype(jnp.bfloat16)
        routed = jnp.dot(picking, returned, preferred_element_type=jnp.float32)
        output = output + route_weights[0][:, route_index][:, None] * routed
    return output.astype(jnp.bfloat16)[None]


def solution(mesh):
    in_specs = (
        P("dp", ("ctx", "exp"), None),
        P("dp", ("ctx", "exp"), None),
        P("dp", ("ctx", "exp"), None),
        P("dp", ("ctx", "exp"), None),
        P("dp", ("ctx", "exp"), None),
        P(),
        P(),
        P("dp", ("ctx", "exp"), None),
        P("dp", ("ctx", "exp"), None),
        P(("ctx", "dp"), "exp", None),
        P(("ctx", "dp"), "exp", None),
        P(("ctx", "dp"), "exp", None),
    )
    out_specs = P("dp", ("ctx", "exp"), None)
    return jax.shard_map(body, mesh=mesh, in_specs=in_specs, out_specs=out_specs, check_vma=False)
```

profile of v0, /device:TPU:0, one launch (start us, length us, event | category | flops | bytes accessed | tf_op | source)
XLA Modules:
  0.0 284.2 jit_solution(2764270609012924020)
XLA Ops:
  6.6 1.2 copy.84
  10.0 0.7 copy-done.1
  10.8 1.6 fusion.28
  12.5 5.1 %all-gather.2 = f32[2,1,8]{2,1,0:T(1,128)S(1)} all-gather(f32[1,1,8]{2,1,0:T(1,128)S(1)} %get-tuple-element.77), channel_id=1, replica_groups=mesh['ctx'=8,'exp'=2,'dp'=2] {'exp'}, dimensions={0}, use_global_device_ids=true | all-gather | bytes 96 | tf_op jit(solution)/shard_map/all_gather | solution.py:87
  17.8 18.8 %all-gather.16.cloned.1.call-done = f32[16,128,128]{2,1,0:T(8,128)} async-done(((f32[8,128,128]{2,1,0:T(8,128)}), f32[16,128,128]{2,1,0:T(8,128)}) %all-gather.16.cloned.1.call-update) | async-done | bytes 1048592 | tf_op jit(solution)/shard_map/all_gather | solution.py:88
  36.6 6.3 %fusion.23 = f32[8,1,128,128]{3,1,2,0:T(1,128)} fusion(f32[2,8,1,1]{0,2,3,1:T(1,128)S(1)} %copy.106, f32[2,8,128,128]{3,2,1,0:T(8,128)} %bitcast.128), kind=kOutput, calls=%fused_computation.26 | convolution fusion | flops 3145728 | bytes 1572928 | tf_op jit(solution)/shard_map/jh,jhab->hab/dot_general | solution.py:103
  43.0 0.7 all-gather.10.cloned.1.call-update
  45.3 20.5 %all-gather.3 = f32[8,1,8]{2,1,0:T(1,128)S(1)} all-gather(f32[1,1,8]{2,1,0:T(1,128)S(1)} %get-tuple-element.83), channel_id=1, replica_groups=mesh['ctx'=8,'exp'=2,'dp'=2] {'ctx'}, dimensions={0}, use_global_device_ids=true | all-gather | bytes 288 | tf_op jit(solution)/shard_map/all_gather | solution.py:9
  66.1 0.6 reduce-window.6
  67.5 3.8 %fusion.21 = f32[8,1,128,128]{3,1,2,0:T(1,128)S(1)} fusion(f32[2,8,1,1]{0,2,3,1:T(1,128)S(1)} %copy.109, f32[2,8,128,128]{3,2,1,0:T(8,128)S(1)} %bitcast.129), kind=kOutput, calls=%fused_computation.24 | convolution fusion | flops 3145728 | bytes 1572928 | tf_op jit(solution)/shard_map/jh,jhab->hab/dot_general | solution.py:99
  71.3 45.3 %all-gather.18.cloned.1.call-done = f32[64,128,128]{2,1,0:T(8,128)} async-done(((f32[8,128,128]{2,1,0:T(8,128)}), f32[64,128,128]{2,1,0:T(8,128)}) %all-gather.18.cloned.1.call-update) | async-done | bytes 4194320 | tf_op jit(solution)/shard_map/all_gather | solution.py:9
  116.9 0.7 fusion.13
  117.9 0.6 fusion.60
  118.9 0.6 copy-done
  120.2 31.8 %all_to_all.10 = bf16[16,20,1024]{2,1,0:T(8,128)(2,1)S(1)} all-to-all(bf16[16,20,1024]{2,1,0:T(8,128)(2,1)S(1)} %reshape.180), channel_id=1, replica_groups=mesh['ctx'=8,'exp'=2,'dp'=2] {'ctx','dp'}, dimensions={0} | all-to-all | bytes 1310720 | tf_op jit(solution)/shard_map/all_to_all | solution.py:144
  152.1 6.4 %all-gather.10.cloned.1.call-done = bf16[1,1024,1408]{2,1,0:T(8,128)(2,1)} async-done(((bf16[1,512,1408]{2,1,0:T(8,128)(2,1)}), bf16[1,1024,1408]{2,1,0:T(8,128)(2,1)}) %all-gather.10.cloned.1.call-update) | async-done | bytes 2883600 | tf_op jit(solution)/shard_map/all_gather | solution.py:153
  158.5 4.2 %fusion.3 = f32[320,1408]{1,0:T(8,128)} fusion(bf16[320,1024]{1,0:T(8,128)(2,1)S(1)} %reshape.181, bf16[1,1024,1408]{2,1,0:T(8,128)(2,1)} %all-gather.10.cloned.1.call-done), kind=kOutput, calls=%fused_computation.6 | convolution fusion | flops 922746880 | bytes 5341184 | tf_op jit(solution)/shard_map/dot_general | solution.py:151
  162.7 39.2 %all-gather.12.cloned.1.call-done = bf16[1,1024,1408]{2,1,0:T(8,128)(2,1)} async-done(((bf16[1,512,1408]{2,1,0:T(8,128)(2,1)}), bf16[1,1024,1408]{2,1,0:T(8,128)(2,1)}) %all-gather.12.cloned.1.call-update) | async-done | bytes 2883600 | tf_op jit(solution)/shard_map/all_gather | solution.py:158
  201.9 43.4 %all-gather.14.cloned.1.call-done = bf16[1,1024,1408]{2,1,0:T(8,128)(2,1)} async-done(((bf16[1,512,1408]{2,1,0:T(8,128)(2,1)}), bf16[1,1024,1408]{2,1,0:T(8,128)(2,1)}) %all-gather.14.cloned.1.call-update) | async-done | bytes 2883600 | tf_op jit(solution)/shard_map/all_gather | solution.py:164
  245.3 5.5 %fusion.8 = bf16[320,1024]{1,0:T(8,128)(2,1)S(1)} fusion(bf16[1,1024,1408]{2,1,0:T(8,128)(2,1)} %all-gather.14.cloned.1.call-done, bf16[320,1024]{1,0:T(8,128)(2,1)S(1)} %reshape.181, bf16[1,1024,1408]{2,1,0:T(8,128)(2,1)} %all-gather.12.cloned.1.call-done, f32[320,1408]{1,0:T(8,128)} %fusion.3), kind=kOutput, calls=%fused_computation.10 | convolution fusion | flops 1848524800 | bytes 8880128 | tf_op jit(solution)/shard_map/dot_general | solution.py:162
  250.8 1.0 reshape.182
  251.8 5.6 %all-to-all-start.1 = ((bf16[16,20,1024]{2,1,0:T(8,128)(2,1)}), bf16[16,20,1024]{2,1,0:T(8,128)(2,1)S(1)}, u32[]{:S(2)}, u32[]{:S(2)}) async-start(bf16[16,20,1024]{2,1,0:T(8,128)(2,1)} %reshape.182), calls=%async_computation.1 | async-start | bytes 1572864 | tf_op jit(solution)/shard_map/all_to_all | solution.py:168
  257.8 18.3 %all-to-all-done.1 = bf16[16,20,1024]{2,1,0:T(8,128)(2,1)S(1)} async-done(((bf16[16,20,1024]{2,1,0:T(8,128)(2,1)}), bf16[16,20,1024]{2,1,0:T(8,128)(2,1)S(1)}, u32[]{:S(2)}, u32[]{:S(2)}) %all-to-all-start.1) | async-done | bytes 655392 | tf_op jit(solution)/shard_map/all_to_all | solution.py:168
  276.6 1.1 fusion.18
  (92 shorter events, 7.8 us)
Async XLA Ops:
  6.5 1.7 copy-start.5
  6.5 30.1 %all-gather.16.cloned.1.call-start = ((), (), s32[]{:S(2)}) async-start(), calls=%async_computation.5 | async-start | bytes 1572864 | tf_op jit(solution)/shard_map/all_gather | solution.py:88
  8.0 0.9 copy-start.9
  8.4 1.0 copy-start.6
  10.0 0.7 copy-start.1
  10.0 0.8 copy-start.3
  12.5 104.2 %all-gather.18.cloned.1.call-start = ((), (), s32[]{:S(2)}) async-start(), calls=%async_computation.6 | async-start | bytes 4718592 | tf_op jit(solution)/shard_map/all_gather | solution.py:9
  43.0 115.5 %all-gather.10.cloned.1.call-start = ((), (), s32[]{:S(2)}) async-start(), calls=%async_computation.2 | async-start | bytes 4325376 | tf_op jit(solution)/shard_map/all_gather | solution.py:153
  43.7 1.2 copy-start.10
  43.7 158.1 %all-gather.12.cloned.1.call-start = ((), (), s32[]{:S(2)}) async-start(), calls=%async_computation.3 | async-start | bytes 4325376 | tf_op jit(solution)/shard_map/all_gather | solution.py:158
  44.3 23.2 %copy-start.12 = (f32[16,128,128]{2,1,0:T(8,128)S(1)}, f32[16,128,128]{2,1,0:T(8,128)}, u32[]{:S(2)}) copy-start(f32[16,128,128]{2,1,0:T(8,128)} %all-gather.16.cloned.1.call-done) | copy-start | bytes 3145732
  44.3 200.9 %all-gather.14.cloned.1.call-start = ((), (), s32[]{:S(2)}) async-start(), calls=%async_computation.4 | async-start | bytes 4325376 | tf_op jit(solution)/shard_map/all_gather | solution.py:164
  116.9 1.0 copy-start.2
  116.9 1.0 copy-start.4
  118.5 1.0 copy-start
  118.5 0.9 copy-start.7
  118.5 1.1 copy-start.8
  250.7 7.0 %copy-start.11 = (f32[1,128,2]{1,2,0:T(2,128)S(1)}, f32[1,128,2]{1,2,0:T(2,128)}, u32[]{:S(2)}) copy-start(f32[1,128,2]{1,2,0:T(2,128)} %param.22) | copy-start | bytes 3076
  251.8 24.3 %all-to-all-start.1 = ((bf16[16,20,1024]{2,1,0:T(8,128)(2,1)}), bf16[16,20,1024]{2,1,0:T(8,128)(2,1)S(1)}, u32[]{:S(2)}, u32[]{:S(2)}) async-start(bf16[16,20,1024]{2,1,0:T(8,128)(2,1)} %reshape.182), calls=%async_computation.1 | async-start | bytes 1572864 | tf_op jit(solution)/shard_map/all_to_all | solution.py:168
Sparse Core Ops, SparseCore 0:
  12.6 23.9 all-gather.15
  43.1 73.4 all-gather.17
  118.2 40.2 all-gather.9
  159.9 41.9 all-gather.11
  203.3 41.9 all-gather.13
where the time goes:
time: 285 us; the launch traced here: 284 us
  waiting for transfers between devices  173 us (61%)
  blocking collectives  57.4 us (20%)
  matrix products  24.5 us (9%)
  between operations  13.6 us (5%)
  local copies, waits for them, and re-layouts  7.28 us (3%)
  starting transfers between devices  5.78 us (2%)
    all_gather x1, waiting for transfers between devices, carried_in(): gathered = jax.tree.map(lambda a: lax.all_gather(a, axis), part)  45.3 us
    all_gather x1, waiting for transfers between devices, body(): lax.all_gather(w_down, 'exp', axis=1, tiled=True)[0]  43.4 us
    all_gather x1, waiting for transfers between devices, body(): lax.all_gather(w_up, 'exp', axis=1, tiled=True)[0]  39.2 us
    all_to_all x1, blocking collectives, body(): lax.all_to_all(outgoing.reshape(expert_count, capacity, model_width), ('c...  31.8 us
    all_gather x1, blocking collectives, carried_in(): gathered = jax.tree.map(lambda a: lax.all_gather(a, axis), part)  20.5 us
    all_gather x1, waiting for transfers between devices, body(): lax.all_gather(block_summary[None], 'exp', axis=0, tiled=True)  18.8 us
    all_to_all x1, waiting for transfers between devices, body(): lax.all_to_all(expert_out.reshape(expert_count, capacity, model_width), (...  18.3 us
    all_gather x1, waiting for transfers between devices, body(): lax.all_gather(w_gate, 'exp', axis=1, tiled=True)[0]  6.36 us
  transfers between devices with their start and end apart: 6, of which 6 were waited for; matrix products, arithmetic and copies ran while one was open for 5% of the time, Pallas kernels for 0%

commit v1 on v0

--- a/solution.py
+++ b/solution.py
@@ -48,6 +48,18 @@
     w_up,
     w_down,
 ):
+    owner_axes = ("ctx", "dp")
+    gather_axis = "exp"
+    shards = (w_gate, w_up, w_down)
+    if lax.axis_size("exp") == 2 and lax.axis_size("dp") == 2:
+        owner_axes = ("ctx", "exp")
+        gather_axis = "dp"
+        shards = tuple(
+            lax.ppermute(w, ("exp", "dp"), [(0, 0), (1, 2), (2, 1), (3, 3)]) for w in shards
+        )
+    full_gate, full_up, full_down = (
+        lax.all_gather(w, gather_axis, axis=1, tiled=True)[0] for w in shards
+    )
     tok_rows = hidden_in.shape[1]
     model_width = hidden_in.shape[2]
     head_count = log_decay.shape[2]
@@ -143,31 +155,31 @@
     outgoing = jnp.dot(placing, normed, preferred_element_type=jnp.float32).astype(jnp.bfloat16)
     arrived = lax.all_to_all(
         outgoing.reshape(expert_count, capacity, model_width),
-        ("ctx", "dp"),
+        owner_axes,
         split_axis=0,
         concat_axis=0,
         tiled=True,
     ).reshape(slot_count, model_width)
     gate_next = jnp.dot(
         arrived,
-        lax.all_gather(w_gate, "exp", axis=1, tiled=True)[0],
+        full_gate,
         preferred_element_type=jnp.float32,
     )
     up_next = jnp.dot(
         arrived,
-        lax.all_gather(w_up, "exp", axis=1, tiled=True)[0],
+        full_up,
         preferred_element_type=jnp.float32,
     )
     hidden = (jax.nn.silu(gate_next) * up_next).astype(jnp.bfloat16)
     expert_out = lax.dot_general(
         hidden,
-        lax.all_gather(w_down, "exp", axis=1, tiled=True)[0],
+        full_down,
         (((1,), (1,)), ((), ())),
         preferred_element_type=jnp.float32,
     ).astype(jnp.bfloat16)
     returned = lax.all_to_all(
         expert_out.reshape(expert_count, capacity, model_width),
-        ("ctx", "dp"),
+        owner_axes,
         split_axis=0,
         concat_axis=0,
         tiled=True,

time: 285 us -> 202 us (0.71)
  waiting for transfers between devices: 173 us -> 73.3 us
  local copies, waits for them, and re-layouts: 7.28 us -> 13.7 us
  starting transfers between devices: 5.78 us -> 11.4 us
  matrix products: 24.5 us -> 27.4 us
    all_gather x3, waiting for transfers between devices: 88.9 us -> 0.02 us  [body(): lax.all_gather(w, gather_axis, axis=1, tiled=True)[0]]
    all_gather x1, waiting for transfers between devices: 45.3 us -> 34.7 us  [carried_in(): gathered = jax.tree.map(lambda a: lax.all_gather(a, axis), part)]
    ppermute x0 -> x3, starting transfers between devices: none -> 6.19 us  [body(): lax.ppermute(w, ('exp', 'dp'), [(0, 0), (1, 2), (2, 1), (3, 3)])]
    unnamed x34, local copies, waits for them, and re-layouts: 4.12 us -> 9.86 us
  transfers between devices with their start and end apart: 6 -> 9, of which waited for: 6 -> 3; matrix products, arithmetic and copies ran while one was open for 5% -> 8% of each run, Pallas kernels for 0% -> 0%
where the time goes in v1:
time: 202 us; the launch traced here: 201 us
  waiting for transfers between devices  73.3 us (36%)
  blocking collectives  59.1 us (29%)
  matrix products  27.4 us (14%)
  local copies, waits for them, and re-layouts  13.7 us (7%)
  between operations  13.5 us (7%)
  starting transfers between devices  11.4 us (6%)
  other arithmetic  2.23 us (1%)
    all_gather x1, waiting for transfers between devices, carried_in(): gathered = jax.tree.map(lambda a: lax.all_gather(a, axis), part)  34.7 us
    all_to_all x1, blocking collectives, body(): lax.all_to_all(outgoing.reshape(expert_count, capacity, model_width), own...  33.2 us
    all_gather x1, blocking collectives, carried_in(): gathered = jax.tree.map(lambda a: lax.all_gather(a, axis), part)  20.8 us
    all_to_all x1, waiting for transfers between devices, body(): lax.all_to_all(expert_out.reshape(expert_count, capacity, model_width), o...  19.7 us
    all_gather x1, waiting for transfers between devices, body(): lax.all_gather(block_summary[None], 'exp', axis=0, tiled=True)  18.8 us
    unnamed x34, local copies, waits for them, and re-layouts  9.86 us
    dot_general x1, matrix products, body(): jnp.einsum('jh,jhab->hab', inner_coeff, group_sums, precision=lax.Precisi...  6.34 us
    dot_general x1, matrix products, body(): jnp.einsum('jh,jhab->hab', total_coeff, group_sums, precision=lax.Precisi...  6.33 us
  transfers between devices with their start and end apart: 9, of which 3 were waited for; matrix products, arithmetic and copies ran while one was open for 8% of the time, Pallas kernels for 0%

profile of v1, /device:TPU:0, one launch (start us, length us, event | category | flops | bytes accessed | tf_op | source)
XLA Modules:
  0.0 200.8 jit_solution(4667740716611415212)
XLA Ops:
  7.6 1.1 copy.84
  8.8 1.1 copy.87
  9.9 1.0 copy.117
  13.2 1.6 fusion.29
  14.9 5.1 %all-gather.2 = f32[2,1,8]{2,1,0:T(1,128)S(1)} all-gather(f32[1,1,8]{2,1,0:T(1,128)S(1)} %get-tuple-element.77), channel_id=1, replica_groups=mesh['ctx'=8,'exp'=2,'dp'=2] {'exp'}, dimensions={0}, use_global_device_ids=true | all-gather | bytes 96 | tf_op jit(solution)/shard_map/all_gather | solution.py:99
  20.3 18.8 %all-gather.16.cloned.1.call-done = f32[16,128,128]{2,1,0:T(8,128)} async-done(((f32[8,128,128]{2,1,0:T(8,128)}), f32[16,128,128]{2,1,0:T(8,128)}) %all-gather.16.cloned.1.call-update) | async-done | bytes 1048592 | tf_op jit(solution)/shard_map/all_gather | solution.py:100
  39.0 6.3 %fusion.24 = f32[8,1,128,128]{3,1,2,0:T(1,128)} fusion(f32[2,8,1,1]{0,2,3,1:T(1,128)S(1)} %copy.106, f32[2,8,128,128]{3,2,1,0:T(8,128)} %bitcast.128), kind=kOutput, calls=%fused_computation.27 | convolution fusion | flops 3145728 | bytes 1572928 | tf_op jit(solution)/shard_map/jh,jhab->hab/dot_general | solution.py:115
  45.4 2.0 %collective-permute-start.1 = (bf16[1,512,1408]{2,1,0:T(8,128)(2,1)}, bf16[1,512,1408]{2,1,0:T(8,128)(2,1)S(1)}, u32[]{:S(2)}, u32[]{:S(2)}) collective-permute-start(bf16[1,512,1408]{2,1,0:T(8,128)(2,1)} %param.24), channel_id=1, source_target_pairs={{0,0},{1,2},{2,1},{3,3},{4,4},{5,6},{6,5},{7,7},{8,8},{9,10},{10,9... | collective-permute-start | bytes 4325384 | tf_op jit(solution)/shard_map/ppermute | solution.py:58
  47.5 1.1 copy-done.1
  48.6 2.0 %collective-permute-start = (bf16[1,512,1408]{2,1,0:T(8,128)(2,1)}, bf16[1,512,1408]{2,1,0:T(8,128)(2,1)S(1)}, u32[]{:S(2)}, u32[]{:S(2)}) collective-permute-start(bf16[1,512,1408]{2,1,0:T(8,128)(2,1)} %param.23), channel_id=1, source_target_pairs={{0,0},{1,2},{2,1},{3,3},{4,4},{5,6},{6,5},{7,7},{8,8},{9,10},{10,9... | collective-permute-start | bytes 4325384 | tf_op jit(solution)/shard_map/ppermute | solution.py:58
  50.7 1.1 copy-done.2
  51.9 2.1 %collective-permute-start.2 = (bf16[1,512,1408]{2,1,0:T(8,128)(2,1)}, bf16[1,512,1408]{2,1,0:T(8,128)(2,1)S(1)}, u32[]{:S(2)}, u32[]{:S(2)}) collective-permute-start(bf16[1,512,1408]{2,1,0:T(8,128)(2,1)} %param.25), channel_id=1, source_target_pairs={{0,0},{1,2},{2,1},{3,3},{4,4},{5,6},{6,5},{7,7},{8,8},{9,10},{10,9... | collective-permute-start | bytes 4325384 | tf_op jit(solution)/shard_map/ppermute | solution.py:58
  55.8 20.8 %all-gather.3 = f32[8,1,8]{2,1,0:T(1,128)S(1)} all-gather(f32[1,1,8]{2,1,0:T(1,128)S(1)} %get-tuple-element.83), channel_id=1, replica_groups=mesh['ctx'=8,'exp'=2,'dp'=2] {'ctx'}, dimensions={0}, use_global_device_ids=true | all-gather | bytes 288 | tf_op jit(solution)/shard_map/all_gather | solution.py:9
  76.8 6.3 %fusion.22 = f32[8,1,128,128]{3,1,2,0:T(1,128)} fusion(f32[2,8,1,1]{0,2,3,1:T(1,128)S(1)} %copy.109, f32[2,8,128,128]{3,2,1,0:T(8,128)} %bitcast.129), kind=kOutput, calls=%fused_computation.25 | convolution fusion | flops 3145728 | bytes 1572928 | tf_op jit(solution)/shard_map/jh,jhab->hab/dot_general | solution.py:111
  83.2 1.1 copy-done.3
  84.3 34.7 %all-gather.18.cloned.1.call-done = f32[64,128,128]{2,1,0:T(8,128)} async-done(((f32[8,128,128]{2,1,0:T(8,128)}), f32[64,128,128]{2,1,0:T(8,128)}) %all-gather.18.cloned.1.call-update) | async-done | bytes 4194320 | tf_op jit(solution)/shard_map/all_gather | solution.py:9
  119.1 1.0 copy-done.8
  123.1 33.2 %all_to_all.10 = bf16[16,20,1024]{2,1,0:T(8,128)(2,1)S(1)} all-to-all(bf16[16,20,1024]{2,1,0:T(8,128)(2,1)S(1)} %reshape.180), channel_id=1, replica_groups=mesh['ctx'=8,'exp'=2,'dp'=2] {'ctx','exp'}, dimensions={0} | all-to-all | bytes 1310720 | tf_op jit(solution)/shard_map/all_to_all | solution.py:156
  156.5 4.5 %fusion.2 = f32[320,1408]{1,0:T(8,128)} fusion(bf16[320,1024]{1,0:T(8,128)(2,1)S(1)} %reshape.181, bf16[1,1024,1408]{2,1,0:T(8,128)(2,1)} %all-gather.12.cloned.1.call-done), kind=kOutput, calls=%fused_computation.4 | convolution fusion | flops 922746880 | bytes 5341184 | tf_op jit(solution)/shard_map/dot_general | solution.py:168
  161.0 5.5 %fusion.6 = bf16[320,1024]{1,0:T(8,128)(2,1)S(1)} fusion(bf16[1,1024,1408]{2,1,0:T(8,128)(2,1)} %all-gather.14.cloned.1.call-done, f32[320,1408]{1,0:T(8,128)} %fusion.2, bf16[320,1024]{1,0:T(8,128)(2,1)S(1)} %reshape.181, bf16[1,1024,1408]{2,1,0:T(8,128)(2,1)} %all-gather.10.cloned.1.call-done), kind=kOutput, calls=%fused_computation.10 | convolution fusion | flops 1848524800 | bytes 8880128 | tf_op jit(solution)/shard_map/dot_general | solution.py:174
  166.5 1.0 reshape.182
  167.5 5.0 %all-to-all-start.1 = ((bf16[16,20,1024]{2,1,0:T(8,128)(2,1)}), bf16[16,20,1024]{2,1,0:T(8,128)(2,1)S(1)}, u32[]{:S(2)}, u32[]{:S(2)}) async-start(bf16[16,20,1024]{2,1,0:T(8,128)(2,1)} %reshape.182), calls=%async_computation.1 | async-start | bytes 1572864 | tf_op jit(solution)/shard_map/all_to_all | solution.py:180
  172.9 19.7 %all-to-all-done.1 = bf16[16,20,1024]{2,1,0:T(8,128)(2,1)S(1)} async-done(((bf16[16,20,1024]{2,1,0:T(8,128)(2,1)}), bf16[16,20,1024]{2,1,0:T(8,128)(2,1)S(1)}, u32[]{:S(2)}, u32[]{:S(2)}) %all-to-all-start.1) | async-done | bytes 655392 | tf_op jit(solution)/shard_map/all_to_all | solution.py:180
  193.2 1.1 fusion.16
  (98 shorter events, 9.7 us)
Async XLA Ops:
  6.5 32.5 %all-gather.16.cloned.1.call-start = ((), (), s32[]{:S(2)}) async-start(), calls=%async_computation.5 | async-start | bytes 1572864 | tf_op jit(solution)/shard_map/all_gather | solution.py:100
  12.4 0.7 copy-start.4
  12.4 0.8 copy-start.6
  14.9 104.1 %all-gather.18.cloned.1.call-start = ((), (), s32[]{:S(2)}) async-start(), calls=%async_computation.6 | async-start | bytes 4718592 | tf_op jit(solution)/shard_map/all_gather | solution.py:9
  45.4 8.6 %copy-start.11 = (s32[1,128,2]{1,2,0:T(2,128)S(1)}, s32[1,128,2]{1,2,0:T(2,128)}, u32[]{:S(2)}) copy-start(s32[1,128,2]{1,2,0:T(2,128)} %param.21) | copy-start | bytes 3076
  45.4 111.1 %all-gather.12.cloned.1.call-start = ((), (), s32[]{:S(2)}) async-start(), calls=%async_computation.3 | async-start | bytes 4325376 | tf_op jit(solution)/shard_map/all_gather | solution.py:61
  45.4 2.0 %collective-permute-start.1 = (bf16[1,512,1408]{2,1,0:T(8,128)(2,1)}, bf16[1,512,1408]{2,1,0:T(8,128)(2,1)S(1)}, u32[]{:S(2)}, u32[]{:S(2)}) collective-permute-start(bf16[1,512,1408]{2,1,0:T(8,128)(2,1)} %param.24), channel_id=1, source_target_pairs={{0,0},{1,2},{2,1},{3,3},{4,4},{5,6},{6,5},{7,7},{8,8},{9,10},{10,9... | collective-permute-start | bytes 4325384 | tf_op jit(solution)/shard_map/ppermute | solution.py:58
  47.5 1.1 copy-start.1
  48.6 112.4 %all-gather.10.cloned.1.call-start = ((), (), s32[]{:S(2)}) async-start(), calls=%async_computation.2 | async-start | bytes 4325376 | tf_op jit(solution)/shard_map/all_gather | solution.py:61
  48.6 2.0 %collective-permute-start = (bf16[1,512,1408]{2,1,0:T(8,128)(2,1)}, bf16[1,512,1408]{2,1,0:T(8,128)(2,1)S(1)}, u32[]{:S(2)}, u32[]{:S(2)}) collective-permute-start(bf16[1,512,1408]{2,1,0:T(8,128)(2,1)} %param.23), channel_id=1, source_target_pairs={{0,0},{1,2},{2,1},{3,3},{4,4},{5,6},{6,5},{7,7},{8,8},{9,10},{10,9... | collective-permute-start | bytes 4325384 | tf_op jit(solution)/shard_map/ppermute | solution.py:58
  50.7 1.1 copy-start.2
  51.8 109.2 %all-gather.14.cloned.1.call-start = ((), (), s32[]{:S(2)}) async-start(), calls=%async_computation.4 | async-start | bytes 4325376 | tf_op jit(solution)/shard_map/all_gather | solution.py:61
  51.9 31.3 %collective-permute-start.2 = (bf16[1,512,1408]{2,1,0:T(8,128)(2,1)}, bf16[1,512,1408]{2,1,0:T(8,128)(2,1)S(1)}, u32[]{:S(2)}, u32[]{:S(2)}) collective-permute-start(bf16[1,512,1408]{2,1,0:T(8,128)(2,1)} %param.25), channel_id=1, source_target_pairs={{0,0},{1,2},{2,1},{3,3},{4,4},{5,6},{6,5},{7,7},{8,8},{9,10},{10,9... | collective-permute-start | bytes 4325384 | tf_op jit(solution)/shard_map/ppermute | solution.py:58
  83.2 1.1 copy-start.3
  119.0 1.0 copy-start.8
  119.1 1.7 copy-start.5
  119.1 1.7 copy-start.7
  121.4 1.0 copy-start
  121.4 0.9 copy-start.9
  121.4 1.1 copy-start.10
  166.5 6.4 %copy-start.12 = (f32[1,128,2]{1,2,0:T(2,128)S(1)}, f32[1,128,2]{1,2,0:T(2,128)}, u32[]{:S(2)}) copy-start(f32[1,128,2]{1,2,0:T(2,128)} %param.22) | copy-start | bytes 3076
  167.5 25.1 %all-to-all-start.1 = ((bf16[16,20,1024]{2,1,0:T(8,128)(2,1)}), bf16[16,20,1024]{2,1,0:T(8,128)(2,1)S(1)}, u32[]{:S(2)}, u32[]{:S(2)}) async-start(bf16[16,20,1024]{2,1,0:T(8,128)(2,1)} %reshape.182), calls=%async_computation.1 | async-start | bytes 1572864 | tf_op jit(solution)/shard_map/all_to_all | solution.py:180
Sparse Core Ops, SparseCore 0:
  15.0 23.9 all-gather.15
  45.5 73.4 all-gather.17
  120.6 9.9 all-gather.11
  132.0 12.8 all-gather.9
  146.3 12.8 all-gather.13

commit v2 on v0

--- a/solution.py
+++ b/solution.py
@@ -1,6 +1,10 @@
+import functools
+
 import jax
 import jax.numpy as jnp
 from jax import lax
+from jax.experimental import pallas as pl
+from jax.experimental.pallas import tpu as pltpu
 from jax.sharding import PartitionSpec as P
 
 
@@ -180,6 +184,570 @@
     return output.astype(jnp.bfloat16)[None]
 
 
+MESH = pl.DeviceIdType.MESH
+BF16 = jnp.bfloat16
+F32 = jnp.float32
+TILE = 16
+
+
+def iota(shape, dim):
+    return lax.broadcasted_iota(jnp.int32, shape, dim)
+
+
+def dot(a, b, contract=((1,), (0,)), precision=None):
+    return lax.dot_general(
+        a, b, (contract, ((), ())), precision=precision, preferred_element_type=F32
+    )
+
+
+def fused_kernel(
+    geo,
+    hid,
+    q,
+    k,
+    v,
+    ld,
+    rgain,
+    ngain,
+    inv,
+    routes,
+    rweights,
+    wg,
+    wu,
+    wd,
+    out,
+    wgb,
+    wub,
+    wdb,
+    sum_send,
+    sum_recv,
+    dec_send,
+    dec_recv,
+    ent_send,
+    ent_recv,
+    disp_main,
+    disp_rem,
+    xall,
+    xin_rem,
+    hidden,
+    eo_main,
+    orem,
+    eo_rem,
+    ret_main,
+    ret_rem,
+    qrot,
+    krot,
+    resid,
+    w_local,
+    w_swap_send,
+    w_swap_recv,
+    w_sib_send,
+    w_sib_recv,
+    x_send,
+    x_recv,
+):
+    ctx_n, exp_n, cap = geo
+    nb = ctx_n * exp_n
+    rows, width = hid.shape
+    heads = ld.shape[1]
+    hd = width // heads
+    ff = wg.shape[1]
+    half = wg.shape[0]
+    rem_n = cap - TILE
+    fold = TILE // rem_n
+    fw = width // fold
+    rp = width // nb
+    x = lax.axis_index("exp")
+    c = lax.axis_index("dp")
+    me = lax.axis_index("ctx") * exp_n + x
+    stays = c == x
+    moves = c != x
+
+    def peer(index):
+        return {"ctx": index // exp_n, "exp": index % exp_n}
+
+    sibling = {"dp": 1 - c}
+    partner = {"exp": c, "dp": x}
+
+    barrier = pltpu.get_barrier_semaphore()
+
+    def greet(d, carry):
+        pl.semaphore_signal(
+            barrier, inc=1, device_id=peer(lax.rem(me + d, nb)), device_id_type=MESH
+        )
+        return carry
+
+    lax.fori_loop(1, nb, greet, 0)
+    pl.semaphore_signal(barrier, inc=1, device_id=sibling, device_id_type=MESH)
+
+    @pl.when(moves)
+    def _():
+        pl.semaphore_signal(barrier, inc=1, device_id=partner, device_id_type=MESH)
+        pl.semaphore_wait(barrier, nb + 1)
+
+    @pl.when(stays)
+    def _():
+        pl.semaphore_wait(barrier, nb)
+
+    chunks = []
+    for array, (src, buf) in enumerate(((wg, wgb), (wu, wub), (wd, wdb))):
+        pieces = 4 if array == 2 else 2
+        step = half // pieces
+        for piece in range(pieces):
+            chunks.append((src, buf, piece * step, step, array))
+
+    def place(buf, owner, start, step):
+        return buf.at[pl.ds(pl.multiple_of(owner * half + start, TILE), step)]
+
+    def swap_copy(i):
+        src, buf, start, step, _ = chunks[i]
+        return pltpu.make_async_remote_copy(
+            src_ref=src.at[pl.ds(start, step)],
+            dst_ref=place(buf, x, start, step),
+            send_sem=w_swap_send.at[i],
+            recv_sem=w_swap_recv.at[i],
+            device_id=partner,
+            device_id_type=MESH,
+        )
+
+    def swap_arrival(i):
+        src, buf, start, step, _ = chunks[i]
+        return pltpu.make_async_remote_copy(
+            src_ref=src.at[pl.ds(start, step)],
+            dst_ref=place(buf, c, start, step),
+            send_sem=w_swap_send.at[i],
+            recv_sem=w_swap_recv.at[i],
+            device_id=partner,
+            device_id_type=MESH,
+        )
+
+    def sib_copy(i, own):
+        src, buf, start, step, _ = chunks[i]
+        mine = place(buf, c, start, step)
+        return pltpu.make_async_remote_copy(
+            src_ref=src.at[pl.ds(start, step)] if own else mine,
+            dst_ref=mine,
+            send_sem=w_sib_send.at[i],
+            recv_sem=w_sib_recv.at[i],
+            device_id=sibling,
+            device_id_type=MESH,
+        )
+
+    def sib_arrival(i):
+        src, buf, start, step, _ = chunks[i]
+        return pltpu.make_async_remote_copy(
+            src_ref=src.at[pl.ds(start, step)],
+            dst_ref=place(buf, 1 - c, start, step),
+            send_sem=w_sib_send.at[i],
+            recv_sem=w_sib_recv.at[i],
+            device_id=sibling,
+            device_id_type=MESH,
+        )
+
+    def local_copy(i):
+        src, buf, start, step, _ = chunks[i]
+        return pltpu.make_async_copy(
+            src.at[pl.ds(start, step)], place(buf, c, start, step), w_local.at[i]
+        )
+
+    @pl.when(moves)
+    def _():
+        for i in range(len(chunks)):
+            swap_copy(i).start()
+
+    @pl.when(stays)
+    def _():
+        for i in range(len(chunks)):
+            sib_copy(i, True).start()
+            local_copy(i).start()
+
+    def hand_on(array):
+        @pl.when(moves)
+        def _():
+            for i in range(len(chunks)):
+                if chunks[i][4] == array:
+                    swap_arrival(i).wait_recv()
+                    sib_copy(i, False).start()
+
+    def take(array):
+        @pl.when(stays)
+        def _():
+            for i in range(len(chunks)):
+                if chunks[i][4] == array:
+                    local_copy(i).wait()
+
+        for i in range(len(chunks)):
+            if chunks[i][4] == array:
+                sib_arrival(i).wait_recv()
+
+    def exchange(kind, src, dst, n):
+        def at(ref, index):
+            return ref.at[pl.ds(pl.multiple_of(index * n, n), n)]
+
+        def copy(d, landing):
+            dest = lax.rem(me + d, nb)
+            return pltpu.make_async_remote_copy(
+                src_ref=at(src, dest),
+                dst_ref=at(dst, landing),
+                send_sem=x_send.at[kind, d],
+                recv_sem=x_recv.at[kind, d],
+                device_id=peer(dest),
+                device_id_type=MESH,
+            )
+
+        def start():
+            def one(d, carry):
+                copy(d, me).start()
+                return carry
+
+            lax.fori_loop(1, nb, one, 0)
+
+        def arrive():
+            def one(d, carry):
+                copy(d, lax.rem(me + nb - d, nb)).wait_recv()
+                return carry
+
+            lax.fori_loop(1, nb, one, 0)
+
+        def sent():
+            def one(d, carry):
+                copy(d, me).wait_send()
+                return carry
+
+            lax.fori_loop(1, nb, one, 0)
+
+        own = pl.ds(pl.multiple_of(me * n, n), n)
+        return start, arrive, sent, own
+
+    lane = iota((rows, hd), 1)
+    position = (me * rows + iota((rows, hd), 0)).astype(F32)
+    angle = position * inv[...]
+    cosine = jnp.cos(angle)
+    sine = jnp.where(lane < hd // 2, -1.0, 1.0) * jnp.sin(angle)
+    causal = iota((rows, rows), 0) >= iota((rows, rows), 1)
+    lower = causal.astype(F32)
+    upper = (iota((rows, rows), 0) <= iota((rows, rows), 1)).astype(F32)
+    decay = ld[...]
+    total = dot(lower, decay, precision=lax.Precision.HIGHEST)
+    total_t = dot(decay.T, upper, precision=lax.Precision.HIGHEST)
+    last_t = total_t[:, rows - 1 : rows]
+    dec_send[...] = jnp.broadcast_to(jnp.exp(last_t), dec_send.shape)
+    for h in range(heads):
+        cols = slice(h * hd, (h + 1) * hd)
+        q_h = q[:, cols].astype(F32)
+        k_h = k[:, cols].astype(F32)
+        q_h = (q_h * cosine + pltpu.roll(q_h, hd // 2, 1) * sine) * hd ** (-0.5)
+        k_h = (k_h * cosine + pltpu.roll(k_h, hd // 2, 1) * sine).astype(BF16)
+        qrot[:, cols] = q_h.astype(BF16)
+        krot[:, cols] = k_h
+        column = total[:, h : h + 1]
+        scaled = k_h.astype(F32) * jnp.exp(total[rows - 1 : rows, h : h + 1] - column)
+        scaled = scaled.T
+        coarse = scaled.astype(BF16)
+        fine = (scaled - coarse.astype(F32)).astype(BF16)
+        v_h = v[:, cols]
+        sum_send[cols, :] = (dot(coarse, v_h) + dot(fine, v_h)).astype(BF16)
+
+    start_s, arrive_s, sent_s, own_s = exchange(0, sum_send, sum_recv, rp)
+
+    def dec_copy(d, landing):
+        dest = lax.rem(me + d, nb)
+        return pltpu.make_async_remote_copy(
+            src_ref=dec_send,
+            dst_ref=dec_recv.at[landing],
+            send_sem=x_send.at[1, d],
+            recv_sem=x_recv.at[1, d],
+            device_id=peer(dest),
+            device_id_type=MESH,
+        )
+
+    def dec_start(d, carry):
+        dec_copy(d, me).start()
+        return carry
+
+    def dec_arrive(d, carry):
+        dec_copy(d, lax.rem(me + nb - d, nb)).wait_recv()
+        return carry
+
+    def dec_sent(d, carry):
+        dec_copy(d, me).wait_send()
+        return carry
+
+    lax.fori_loop(1, nb, dec_start, 0)
+    start_s()
+    sum_recv[own_s, :] = sum_send[own_s, :]
+    dec_recv[me] = dec_send[...]
+
+    for h in range(heads):
+        cols = slice(h * hd, (h + 1) * hd)
+        spread = total[:, h : h + 1] - total_t[h : h + 1, :]
+        scores = dot(qrot[:, cols], krot[:, cols], ((1,), (1,)))
+        weights = jnp.where(causal, scores * jnp.exp(jnp.where(causal, spread, 0.0)), 0.0)
+        resid[:, cols] = dot(weights.astype(BF16), v[:, cols])
+
+    lax.fori_loop(1, nb, dec_arrive, 0)
+    arrive_s()
+    head = (me * rp) // hd
+    state = jnp.zeros((rp, hd), F32)
+    for b in range(nb):
+        part = slice(b * rp, (b + 1) * rp)
+        ent_send[part, :] = state.astype(BF16)
+        if b < nb - 1:
+            state = dec_recv[b, pl.ds(head, 1), :] * state + sum_recv[part, :].astype(F32)
+    start_e, arrive_e, sent_e, own_e = exchange(2, ent_send, ent_recv, rp)
+    start_e()
+    ent_recv[own_e, :] = ent_send[own_e, :]
+
+    r0 = routes[:, 0:1]
+    r1 = routes[:, 1:2]
+    lanes = iota((rows, 128), 1)
+    hits = ((r0 == lanes) | (r1 == lanes)).astype(BF16)
+    strict = (iota((rows, rows), 0) > iota((rows, rows), 1)).astype(BF16)
+    before = dot(strict, hits)
+    slots = iota((rows, nb * TILE), 1).astype(F32)
+    pick_main, pick_rem = [], []
+    for r in (r0, r1):
+        rank = jnp.sum(jnp.where(r == lanes, before, 0.0), axis=1, keepdims=True)
+        base = r.astype(F32) * TILE + rank
+        in_main = jnp.where(rank < TILE, base, -1.0)
+        in_rem = jnp.where(rank < TILE, -1.0e6, base - TILE)
+        pick_main.append((in_main == slots).astype(F32))
+        pick_rem.append([(in_rem + f * rem_n == slots).astype(F32) for f in range(fold)])
+    put_main = (pick_main[0] + pick_main[1]).T.astype(BF16)
+    put_rem = [(pick_rem[0][f] + pick_rem[1][f]).T.astype(BF16) for f in range(fold)]
+    pick_main = [p.astype(BF16) for p in pick_main]
+    pick_rem = [[p.astype(BF16) for p in ps] for ps in pick_rem]
+
+    hand_on(0)
+
+    arrive_e()
+    square = jnp.zeros((rows, 1), F32)
+    for h in range(heads):
+        cols = slice(h * hd, (h + 1) * hd)
+        carried = dot(qrot[:, cols], ent_recv[cols, :])
+        got = resid[:, cols] + jnp.exp(total[:, h : h + 1]) * carried
+        got = got - jnp.mean(got, axis=1, keepdims=True)
+        variance = jnp.mean(got * got, axis=1, keepdims=True)
+        got = got * lax.rsqrt(variance + 1e-05)
+        got = hid[:, cols].astype(F32) + rgain[:, cols] * got
+        resid[:, cols] = got
+        square = square + jnp.sum(got * got, axis=1, keepdims=True)
+    normed = (resid[...] * lax.rsqrt(square / width + 1e-06) * ngain[...]).astype(BF16)
+
+    disp_main[...] = dot(put_main, normed).astype(BF16)
+    folded = jnp.zeros((nb * TILE, fw), F32)
+    for f in range(fold):
+        folded = folded + dot(put_rem[f], normed[:, f * fw : (f + 1) * fw])
+    disp_rem[...] = folded.astype(BF16)
+    start_m, arrive_m, sent_m, own_m = exchange(3, disp_main, xall, TILE)
+    start_r, arrive_r, sent_r, own_r = exchange(4, disp_rem, xin_rem, TILE)
+    start_m()
+    start_r()
+    xall[own_m, :] = disp_main[own_m, :]
+    xin_rem[own_r, :] = disp_rem[own_r, :]
+
+    hand_on(1)
+    arrive_m()
+    arrive_r()
+    row = iota((nb * rem_n, nb * TILE), 0)
+    spot = (row // rem_n) * TILE + lax.rem(row, rem_n)
+    for f in range(fold):
+        unfold = (iota((nb * rem_n, nb * TILE), 1) == spot + f * rem_n).astype(F32)
+        xall[nb * TILE :, f * fw : (f + 1) * fw] = dot(unfold.astype(BF16), xin_rem[...]).astype(
+            BF16
+        )
+
+    take(0)
+    take(1)
+
+    def gate_up(i, carry):
+        cols = pl.ds(pl.multiple_of(i * 128, 128), 128)
+        both = dot(xall[...], jnp.concatenate([wgb[:, cols], wub[:, cols]], axis=1))
+        gate = both[:, :128]
+        hidden[:, cols] = (gate / (1.0 + jnp.exp(-gate)) * both[:, 128:]).astype(BF16)
+        return carry
+
+    lax.fori_loop(0, ff // 128, gate_up, 0)
+    hand_on(2)
+    take(2)
+    block = 256
+
+    def down(i, carry):
+        cols = pl.ds(pl.multiple_of(i * block, block), block)
+        result = dot(hidden[...], wdb[cols, :], ((1,), (1,))).astype(BF16)
+        eo_main[:, cols] = result[: nb * TILE]
+        orem[:, cols] = result[nb * TILE :]
+        return carry
+
+    lax.fori_loop(0, width // block, down, 0)
+    start_b, arrive_b, sent_b, own_b = exchange(5, eo_main, ret_main, TILE)
+    start_b()
+    ret_main[own_b, :] = eo_main[own_b, :]
+    column = iota((nb * TILE, nb * rem_n), 1)
+    spot = (column // rem_n) * TILE + lax.rem(column, rem_n)
+    folded = jnp.zeros((nb * TILE, fw), F32)
+    for f in range(fold):
+        refold = (iota((nb * TILE, nb * rem_n), 0) == spot + f * rem_n).astype(F32)
+        folded = folded + dot(refold.astype(BF16), orem[:, f * fw : (f + 1) * fw])
+    eo_rem[...] = folded.astype(BF16)
+    start_q, arrive_q, sent_q, own_q = exchange(6, eo_rem, ret_rem, TILE)
+    start_q()
+    ret_rem[own_q, :] = eo_rem[own_q, :]
+
+    @pl.when(moves)
+    def _():
+        for i in range(len(chunks)):
+            swap_copy(i).wait_send()
+            sib_copy(i, False).wait_send()
+
+    @pl.when(stays)
+    def _():
+        for i in range(len(chunks)):
+            sib_copy(i, True).wait_send()
+
+    lax.fori_loop(1, nb, dec_sent, 0)
+    sent_s()
+    sent_e()
+    sent_m()
+    sent_r()
+
+    arrive_b()
+    arrive_q()
+    for f in range(fold):
+        cols = slice(f * fw, (f + 1) * fw)
+        acc = resid[:, cols]
+        for j in range(2):
+            routed = dot(pick_main[j], ret_main[:, cols]) + dot(pick_rem[j][f], ret_rem[...])
+            acc = acc + rweights[:, j : j + 1] * routed
+        out[:, cols] = acc.astype(BF16)
+    sent_b()
+    sent_q()
+
+
+def fused(geo, *args):
+    (
+        hidden_in,
+        queries,
+        keys,
+        values,
+        log_decay,
+        retention_gain,
+        norm_gain,
+        routes,
+        route_weights,
+        w_gate,
+        w_up,
+        w_down,
+    ) = args
+    ctx_n, exp_n, cap = geo
+    nb = ctx_n * exp_n
+    rows, width = hidden_in.shape[1:]
+    heads = log_decay.shape[2]
+    hd = width // heads
+    ff = w_gate.shape[2]
+    rem_n = cap - TILE
+    fw = width * rem_n // TILE
+    rp = width // nb
+    frequencies = 10000.0 ** (-jnp.arange(hd // 2, dtype=F32) / (hd // 2))
+    inverse = jnp.concatenate([frequencies, frequencies])[None]
+    vmem = pl.BlockSpec(memory_space=pltpu.VMEM)
+    hbm = pl.BlockSpec(memory_space=pl.ANY)
+    n_chunks = 8
+    dma = pltpu.SemaphoreType.DMA
+    out = pl.pallas_call(
+        functools.partial(fused_kernel, geo),
+        out_shape=jax.ShapeDtypeStruct((rows, width), BF16),
+        in_specs=[vmem] * 10 + [hbm] * 3,
+        out_specs=vmem,
+        scratch_shapes=[
+            pltpu.VMEM((width, ff), BF16),
+            pltpu.VMEM((width, ff), BF16),
+            pltpu.VMEM((width, ff), BF16),
+            pltpu.VMEM((width, hd), BF16),
+            pltpu.VMEM((width, hd), BF16),
+            pltpu.VMEM((heads, hd), F32),
+            pltpu.VMEM((nb, heads, hd), F32),
+            pltpu.VMEM((width, hd), BF16),
+            pltpu.VMEM((width, hd), BF16),
+            pltpu.VMEM((nb * TILE, width), BF16),
+            pltpu.VMEM((nb * TILE, fw), BF16),
+            pltpu.VMEM((nb * cap, width), BF16),
+            pltpu.VMEM((nb * TILE, fw), BF16),
+            pltpu.VMEM((nb * cap, ff), BF16),
+            pltpu.VMEM((nb * TILE, width), BF16),
+            pltpu.VMEM((nb * rem_n, width), BF16),
+            pltpu.VMEM((nb * TILE, fw), BF16),
+            pltpu.VMEM((nb * TILE, width), BF16),
+            pltpu.VMEM((nb * TILE, fw), BF16),
+            pltpu.VMEM((rows, width), BF16),
+            pltpu.VMEM((rows, width), BF16),
+            pltpu.VMEM((rows, width), F32),
+            dma((n_chunks,)),
+            dma((n_chunks,)),
+            dma((n_chunks,)),
+            dma((n_chunks,)),
+            dma((n_chunks,)),
+            dma((7, nb)),
+            dma((7, nb)),
+        ],
+        compiler_params=pltpu.CompilerParams(
+            collective_id=0, has_side_effects=True, vmem_limit_bytes=48 * 1024 * 1024
+        ),
+    )(
+        hidden_in[0],
+        queries[0],
+        keys[0],
+        values[0],
+        log_decay[0],
+        retention_gain[None],
+        norm_gain[None],
+        inverse,
+        routes[0],
+        route_weights[0],
+        w_gate[0],
+        w_up[0],
+        w_down[0],
+    )
+    return out[None]
+
+
+def geometry(args):
+    ctx_n, exp_n, dp_n = (lax.axis_size(a) for a in ("ctx", "exp", "dp"))
+    nb = ctx_n * exp_n
+    rows, width = args[0].shape[1:]
+    heads = args[4].shape[2]
+    hd = width // heads
+    top = args[7].shape[2]
+    experts = ctx_n * dp_n
+    cap = (rows * top * 5 + 4 * experts - 1) // (4 * experts)
+    rem_n = cap - TILE
+    fits = (
+        exp_n == 2
+        and dp_n == 2
+        and top == 2
+        and experts <= 128
+        and 0 < rem_n < TILE
+        and TILE % rem_n == 0
+        and (width * rem_n) % (TILE * 128) == 0
+        and nb * rem_n % TILE == 0
+        and hd == 128
+        and rows == 128
+        and heads == 8
+        and width % nb == 0
+        and (width // nb) % TILE == 0
+        and hd % (width // nb) == 0
+        and args[9].shape[2] % 128 == 0
+        and width % 256 == 0
+        and args[9].shape[1] * 2 == width
+    )
+    return (ctx_n, exp_n, cap) if fits else None
+
+
+def layer(*args):
+    geo = geometry(args)
+    return body(*args) if geo is None else fused(geo, *args)
+
+
 def solution(mesh):
     in_specs = (
         P("dp", ("ctx", "exp"), None),
@@ -196,4 +764,4 @@
         P(("ctx", "dp"), "exp", None),
     )
     out_specs = P("dp", ("ctx", "exp"), None)
-    return jax.shard_map(body, mesh=mesh, in_specs=in_specs, out_specs=out_specs, check_vma=False)
+    return jax.shard_map(layer, mesh=mesh, in_specs=in_specs, out_specs=out_specs, check_vma=False)

time: 285 us -> 120 us (0.42)
  waiting for transfers between devices: 173 us -> 0 us
  Pallas kernels: 0 us -> 106 us
  blocking collectives: 57.4 us -> 0 us
  matrix products: 24.5 us -> 0 us
  between operations: 13.6 us -> 0.03 us
  starting transfers between devices: 5.78 us -> 0 us
  local copies, waits for them, and re-layouts: 7.28 us -> 12.3 us
    all_gather x5 -> x0, waiting for transfers between devices: 153 us -> none  [the longest x1 45.3 us: carried_in(): gathered = jax.tree.map(lambda a: lax.all_gather(a, axis), part)]
    pallas_call x0 -> x1, Pallas kernels: none -> 106 us  [fused(): pl.pallas_call(functools.partial(fused_kernel, geo), out_shape=jax.ShapeD...]
    all_to_all x1 -> x0, blocking collectives: 31.8 us -> none  [body(): lax.all_to_all(outgoing.reshape(expert_count, capacity, model_width), ('c...]
    all_gather x2 -> x0, blocking collectives: 25.6 us -> none  [the longest x1 20.5 us: carried_in(): gathered = jax.tree.map(lambda a: lax.all_gather(a, axis), part)]
    dot_general x10 -> x0, matrix products: 24.5 us -> none  [the longest x1 6.35 us: body(): jnp.einsum('jh,jhab->hab', total_coeff, group_sums, precision=lax.Precisi...]
    all_to_all x1 -> x0, waiting for transfers between devices: 18.3 us -> none  [body(): lax.all_to_all(expert_out.reshape(expert_count, capacity, model_width), (...]
    unnamed x34 -> x22, local copies, waits for them, and re-layouts: 4.12 us -> 12.3 us
    all_to_all x1 -> x0, starting transfers between devices: 5.62 us -> none  [body(): lax.all_to_all(expert_out.reshape(expert_count, capacity, model_width), (...]
  transfers between devices with their start and end apart: 6 -> 0, of which waited for: 6 -> 0; matrix products, arithmetic and copies ran while one was open for 5% -> 0% of each run, Pallas kernels for 0% -> 0%
where the time goes in v2:
time: 120 us; the launch traced here: 118 us
  Pallas kernels  106 us (88%)
  local copies, waits for them, and re-layouts  12.3 us (10%)
    pallas_call x1, Pallas kernels, fused(): pl.pallas_call(functools.partial(fused_kernel, geo), out_shape=jax.ShapeD...  106 us
    unnamed x22, local copies, waits for them, and re-layouts  12.3 us

profile of v2, /device:TPU:0, one launch (start us, length us, event | category | flops | bytes accessed | tf_op | source)
XLA Modules:
  0.0 118.2 jit_solution(10154504385396254945)
XLA Ops:
  0.0 0.1 maximum_bitcast_fusion.inv
  0.1 0.8 copy.13
  0.9 0.8 copy.14
  1.7 0.8 copy.15
  2.5 0.0 copy-start
  2.5 1.4 %copy-done = bf16[1,512,1408]{2,1,0:T(8,128)(2,1)S(1)} copy-done((bf16[1,512,1408]{2,1,0:T(8,128)(2,1)S(1)}, bf16[1,512,1408]{2,1,0:T(8,128)(2,1)}, u32[]{:S(2)}) %copy-start) | copy-done | bytes 1441816
  3.8 0.0 copy-start.1
  3.8 1.4 %copy-done.1 = bf16[1,512,1408]{2,1,0:T(8,128)(2,1)S(1)} copy-done((bf16[1,512,1408]{2,1,0:T(8,128)(2,1)S(1)}, bf16[1,512,1408]{2,1,0:T(8,128)(2,1)}, u32[]{:S(2)}) %copy-start.1) | copy-done | bytes 1441816
  5.2 0.0 copy-start.2
  5.2 1.4 %copy-done.2 = bf16[1,512,1408]{2,1,0:T(8,128)(2,1)S(1)} copy-done((bf16[1,512,1408]{2,1,0:T(8,128)(2,1)S(1)}, bf16[1,512,1408]{2,1,0:T(8,128)(2,1)}, u32[]{:S(2)}) %copy-start.2) | copy-done | bytes 1441816
  6.5 0.0 copy-start.3
  6.5 0.9 copy-done.3
  7.5 0.0 copy-start.4
  7.5 0.9 copy-done.4
  8.4 0.0 copy-start.5
  8.4 0.9 copy-done.5
  9.4 0.0 copy-start.6
  9.4 0.9 copy-done.6
  10.3 0.0 copy-start.7
  10.3 0.7 copy-done.7
  11.0 0.0 copy-start.8
  11.0 0.7 copy-done.8
  11.7 105.8 %shard_map.118 = bf16[128,1024]{1,0:T(8,128)(2,1)S(1)} custom-call(bf16[128,1024]{1,0:T(8,128)(2,1)S(1)} %bitcast.22, bf16[128,1024]{1,0:T(8,128)(2,1)S(1)} %bitcast.23, bf16[128,1024]{1,0:T(8,128)(2,1)S(1)} %bitcast.24, bf16[128,1024]{1,0:T(8,128)(2,1)S(1)} %bitcast.25, f32[128,8]{1,0:T(8,128)S(1)} %bitcast.19, f32[1,1024]{1,0:T(1,128)S(1)} %bitcast.26, ...), custom_call_target="tpu_custom_call" | custom-call | tf_op jit(solution)/shard_map/pallas_call | solution.py:657
  117.5 0.7 copy.17
  (1 shorter events, 0.0 us)
Async XLA Ops:
  2.5 1.4 %copy-start = (bf16[1,512,1408]{2,1,0:T(8,128)(2,1)S(1)}, bf16[1,512,1408]{2,1,0:T(8,128)(2,1)}, u32[]{:S(2)}) copy-start(bf16[1,512,1408]{2,1,0:T(8,128)(2,1)} %param.21) | copy-start | bytes 4325380
  3.8 1.4 %copy-start.1 = (bf16[1,512,1408]{2,1,0:T(8,128)(2,1)S(1)}, bf16[1,512,1408]{2,1,0:T(8,128)(2,1)}, u32[]{:S(2)}) copy-start(bf16[1,512,1408]{2,1,0:T(8,128)(2,1)} %param.22) | copy-start | bytes 4325380
  5.2 1.4 %copy-start.2 = (bf16[1,512,1408]{2,1,0:T(8,128)(2,1)S(1)}, bf16[1,512,1408]{2,1,0:T(8,128)(2,1)}, u32[]{:S(2)}) copy-start(bf16[1,512,1408]{2,1,0:T(8,128)(2,1)} %param.23) | copy-start | bytes 4325380
  6.5 0.9 copy-start.3
  7.5 0.9 copy-start.4
  8.4 0.9 copy-start.5
  9.4 0.9 copy-start.6
  10.3 0.7 copy-start.7
  11.0 0.7 copy-start.8

commit v3 on v2

--- a/solution.py
+++ b/solution.py
@@ -1,4 +1,5 @@
 import functools
+import math
 
 import jax
 import jax.numpy as jnp
@@ -202,6 +203,19 @@
 
 def fused_kernel(
     geo,
+    hid_in,
+    q_in,
+    k_in,
+    v_in,
+    ld_in,
+    rgain_in,
+    ngain_in,
+    routes_in,
+    rweights_in,
+    wg,
+    wu,
+    wd,
+    out,
     hid,
     q,
     k,
@@ -209,13 +223,8 @@
     ld,
     rgain,
     ngain,
-    inv,
     routes,
     rweights,
-    wg,
-    wu,
-    wd,
-    out,
     wgb,
     wub,
     wdb,
@@ -225,19 +234,17 @@
     dec_recv,
     ent_send,
     ent_recv,
-    disp_main,
-    disp_rem,
+    disp,
+    xin,
     xall,
-    xin_rem,
     hidden,
-    eo_main,
     orem,
-    eo_rem,
-    ret_main,
-    ret_rem,
+    eo,
+    ret,
     qrot,
     krot,
     resid,
+    in_sem,
     w_local,
     w_swap_send,
     w_swap_recv,
@@ -249,7 +256,7 @@
     ctx_n, exp_n, cap = geo
     nb = ctx_n * exp_n
     rows, width = hid.shape
-    heads = ld.shape[1]
+    heads = ld.shape[0]
     hd = width // heads
     ff = wg.shape[1]
     half = wg.shape[0]
@@ -269,6 +276,25 @@
     sibling = {"dp": 1 - c}
     partner = {"exp": c, "dp": x}
 
+    arguments = [
+        pltpu.make_async_copy(src, dst, in_sem.at[i])
+        for i, (src, dst) in enumerate(
+            (
+                (ld_in, ld),
+                (k_in, k),
+                (v_in, v),
+                (q_in, q),
+                (routes_in, routes),
+                (hid_in, hid),
+                (rgain_in, rgain),
+                (ngain_in, ngain),
+                (rweights_in, rweights),
+            )
+        )
+    ]
+    for argument in arguments:
+        argument.start()
+
     barrier = pltpu.get_barrier_semaphore()
 
     def greet(d, carry):
@@ -283,6 +309,16 @@
     @pl.when(moves)
     def _():
         pl.semaphore_signal(barrier, inc=1, device_id=partner, device_id_type=MESH)
+
+    lane = iota((rows, hd), 1)
+    pair = jnp.where(lane < hd // 2, lane, lane - hd // 2).astype(F32)
+    position = (me * rows + iota((rows, hd), 0)).astype(F32)
+    angle = position * jnp.exp(pair * (-math.log(10000.0) / (hd // 2)))
+    cosine = jnp.cos(angle)
+    sine = jnp.where(lane < hd // 2, -1.0, 1.0) * jnp.sin(angle)
+
+    @pl.when(moves)
+    def _():
         pl.semaphore_wait(barrier, nb + 1)
 
     @pl.when(stays)
@@ -350,35 +386,42 @@
             src.at[pl.ds(start, step)], place(buf, c, start, step), w_local.at[i]
         )
 
-    @pl.when(moves)
-    def _():
-        for i in range(len(chunks)):
-            swap_copy(i).start()
-
-    @pl.when(stays)
-    def _():
-        for i in range(len(chunks)):
-            sib_copy(i, True).start()
-            local_copy(i).start()
-
-    def hand_on(array):
+    def begin(first, last):
         @pl.when(moves)
         def _():
-            for i in range(len(chunks)):
-                if chunks[i][4] == array:
-                    swap_arrival(i).wait_recv()
-                    sib_copy(i, False).start()
-
-    def take(array):
+            for i in range(first, last):
+                swap_copy(i).start()
+
         @pl.when(stays)
         def _():
-            for i in range(len(chunks)):
-                if chunks[i][4] == array:
-                    local_copy(i).wait()
-
-        for i in range(len(chunks)):
-            if chunks[i][4] == array:
-                sib_arrival(i).wait_recv()
+            for i in range(first, last):
+                sib_copy(i, True).start()
+                local_copy(i).start()
+
+    begin(0, 1)
+
+    def chosen(array, group):
+        found = [i for i in range(len(chunks)) if chunks[i][4] == array]
+        if group is None:
+            return found
+        share = len(found) // 2
+        return found[group * share : (group + 1) * share]
+
+    def hand_on(array, group=None):
+        @pl.when(moves)
+        def _():
+            for i in chosen(array, group):
+                swap_arrival(i).wait_recv()
+                sib_copy(i, False).start()
+
+    def take(array, group=None):
+        @pl.when(stays)
+        def _():
+            for i in chosen(array, group):
+                local_copy(i).wait()
+
+        for i in chosen(array, group):
+            sib_arrival(i).wait_recv()
 
     def exchange(kind, src, dst, n):
         def at(ref, index):
@@ -419,17 +462,12 @@
         own = pl.ds(pl.multiple_of(me * n, n), n)
         return start, arrive, sent, own
 
-    lane = iota((rows, hd), 1)
-    position = (me * rows + iota((rows, hd), 0)).astype(F32)
-    angle = position * inv[...]
-    cosine = jnp.cos(angle)
-    sine = jnp.where(lane < hd // 2, -1.0, 1.0) * jnp.sin(angle)
     causal = iota((rows, rows), 0) >= iota((rows, rows), 1)
-    lower = causal.astype(F32)
     upper = (iota((rows, rows), 0) <= iota((rows, rows), 1)).astype(F32)
-    decay = ld[...]
-    total = dot(lower, decay, precision=lax.Precision.HIGHEST)
-    total_t = dot(decay.T, upper, precision=lax.Precision.HIGHEST)
+    for argument in arguments[:4]:
+        argument.wait()
+    total_t = dot(ld[...], upper, precision=lax.Precision.HIGHEST)
+    total = total_t.T
     last_t = total_t[:, rows - 1 : rows]
     dec_send[...] = jnp.broadcast_to(jnp.exp(last_t), dec_send.shape)
     for h in range(heads):
@@ -475,6 +513,7 @@
 
     lax.fori_loop(1, nb, dec_start, 0)
     start_s()
+    begin(1, 2)
     sum_recv[own_s, :] = sum_send[own_s, :]
     dec_recv[me] = dec_send[...]
 
@@ -496,11 +535,17 @@
             state = dec_recv[b, pl.ds(head, 1), :] * state + sum_recv[part, :].astype(F32)
     start_e, arrive_e, sent_e, own_e = exchange(2, ent_send, ent_recv, rp)
     start_e()
+    begin(2, 4)
+    for argument in arguments[4:]:
+        argument.wait()
     ent_recv[own_e, :] = ent_send[own_e, :]
 
-    r0 = routes[:, 0:1]
-    r1 = routes[:, 1:2]
-    lanes = iota((rows, 128), 1)
+    by_position = jnp.concatenate(
+        [routes[...].astype(F32), rweights[...], jnp.zeros((4, rows), F32)], axis=0
+    ).T
+    r0 = by_position[:, 0:1]
+    r1 = by_position[:, 1:2]
+    lanes = iota((rows, 128), 1).astype(F32)
     hits = ((r0 == lanes) | (r1 == lanes)).astype(BF16)
     strict = (iota((rows, rows), 0) > iota((rows, rows), 1)).astype(BF16)
     before = dot(strict, hits)
@@ -508,7 +553,7 @@
     pick_main, pick_rem = [], []
     for r in (r0, r1):
         rank = jnp.sum(jnp.where(r == lanes, before, 0.0), axis=1, keepdims=True)
-        base = r.astype(F32) * TILE + rank
+        base = r * TILE + rank
         in_main = jnp.where(rank < TILE, base, -1.0)
         in_rem = jnp.where(rank < TILE, -1.0e6, base - TILE)
         pick_main.append((in_main == slots).astype(F32))
@@ -517,8 +562,6 @@
     put_rem = [(pick_rem[0][f] + pick_rem[1][f]).T.astype(BF16) for f in range(fold)]
     pick_main = [p.astype(BF16) for p in pick_main]
     pick_rem = [[p.astype(BF16) for p in ps] for ps in pick_rem]
-
-    hand_on(0)
 
     arrive_e()
     square = jnp.zeros((rows, 1), F32)
@@ -534,26 +577,25 @@
         square = square + jnp.sum(got * got, axis=1, keepdims=True)
     normed = (resid[...] * lax.rsqrt(square / width + 1e-06) * ngain[...]).astype(BF16)
 
-    disp_main[...] = dot(put_main, normed).astype(BF16)
+    disp[:, :width] = dot(put_main, normed).astype(BF16)
     folded = jnp.zeros((nb * TILE, fw), F32)
     for f in range(fold):
         folded = folded + dot(put_rem[f], normed[:, f * fw : (f + 1) * fw])
-    disp_rem[...] = folded.astype(BF16)
-    start_m, arrive_m, sent_m, own_m = exchange(3, disp_main, xall, TILE)
-    start_r, arrive_r, sent_r, own_r = exchange(4, disp_rem, xin_rem, TILE)
+    disp[:, width:] = folded.astype(BF16)
+    start_m, arrive_m, sent_m, own_m = exchange(3, disp, xin, TILE)
     start_m()
-    start_r()
-    xall[own_m, :] = disp_main[own_m, :]
-    xin_rem[own_r, :] = disp_rem[own_r, :]
-
+    begin(4, 8)
+    xin[own_m, :] = disp[own_m, :]
+
+    hand_on(0)
     hand_on(1)
     arrive_m()
-    arrive_r()
+    xall[: nb * TILE, :] = xin[:, :width]
     row = iota((nb * rem_n, nb * TILE), 0)
     spot = (row // rem_n) * TILE + lax.rem(row, rem_n)
     for f in range(fold):
         unfold = (iota((nb * rem_n, nb * TILE), 1) == spot + f * rem_n).astype(F32)
-        xall[nb * TILE :, f * fw : (f + 1) * fw] = dot(unfold.astype(BF16), xin_rem[...]).astype(
+        xall[nb * TILE :, f * fw : (f + 1) * fw] = dot(unfold.astype(BF16), xin[:, width:]).astype(
             BF16
         )
 
@@ -568,31 +610,35 @@
         return carry
 
     lax.fori_loop(0, ff // 128, gate_up, 0)
-    hand_on(2)
-    take(2)
-    block = 256
-
-    def down(i, carry):
-        cols = pl.ds(pl.multiple_of(i * block, block), block)
-        result = dot(hidden[...], wdb[cols, :], ((1,), (1,))).astype(BF16)
-        eo_main[:, cols] = result[: nb * TILE]
-        orem[:, cols] = result[nb * TILE :]
-        return carry
-
-    lax.fori_loop(0, width // block, down, 0)
-    start_b, arrive_b, sent_b, own_b = exchange(5, eo_main, ret_main, TILE)
-    start_b()
-    ret_main[own_b, :] = eo_main[own_b, :]
+    groups = 2
+    part_w = half // groups
+    gw = 2 * part_w
+    pw = fw // groups
     column = iota((nb * TILE, nb * rem_n), 1)
     spot = (column // rem_n) * TILE + lax.rem(column, rem_n)
-    folded = jnp.zeros((nb * TILE, fw), F32)
-    for f in range(fold):
-        refold = (iota((nb * TILE, nb * rem_n), 0) == spot + f * rem_n).astype(F32)
-        folded = folded + dot(refold.astype(BF16), orem[:, f * fw : (f + 1) * fw])
-    eo_rem[...] = folded.astype(BF16)
-    start_q, arrive_q, sent_q, own_q = exchange(6, eo_rem, ret_rem, TILE)
-    start_q()
-    ret_rem[own_q, :] = eo_rem[own_q, :]
+    returns = []
+    for g in range(groups):
+        hand_on(2, g)
+        take(2, g)
+
+        def down(i, carry):
+            src = pl.ds(pl.multiple_of(i * half + g * part_w, part_w), part_w)
+            cols = pl.ds(pl.multiple_of(i * part_w, part_w), part_w)
+            result = dot(hidden[...], wdb[src, :], ((1,), (1,))).astype(BF16)
+            eo[g, :, cols] = result[: nb * TILE]
+            orem[:, cols] = result[nb * TILE :]
+            return carry
+
+        lax.fori_loop(0, 2, down, 0)
+        folded = jnp.zeros((nb * TILE, pw), F32)
+        for f in range(fold):
+            refold = (iota((nb * TILE, nb * rem_n), 0) == spot + f * rem_n).astype(F32)
+            folded = folded + dot(refold.astype(BF16), orem[:, f * pw : (f + 1) * pw])
+        eo[g, :, gw:] = folded.astype(BF16)
+        start_b, arrive_b, sent_b, own_b = exchange(4 + g, eo.at[g], ret.at[g], TILE)
+        start_b()
+        ret[g, own_b, :] = eo[g, own_b, :]
+        returns.append((arrive_b, sent_b))
 
     @pl.when(moves)
     def _():
@@ -609,19 +655,22 @@
     sent_s()
     sent_e()
     sent_m()
-    sent_r()
-
-    arrive_b()
-    arrive_q()
-    for f in range(fold):
-        cols = slice(f * fw, (f + 1) * fw)
-        acc = resid[:, cols]
-        for j in range(2):
-            routed = dot(pick_main[j], ret_main[:, cols]) + dot(pick_rem[j][f], ret_rem[...])
-            acc = acc + rweights[:, j : j + 1] * routed
-        out[:, cols] = acc.astype(BF16)
-    sent_b()
-    sent_q()
+
+    for g in range(groups):
+        arrive_b, sent_b = returns[g]
+        arrive_b()
+        for f in range(fold):
+            start = f * pw
+            into = (start // part_w) * half + g * part_w + start % part_w
+            cols = slice(into, into + pw)
+            acc = resid[:, cols]
+            for j in range(2):
+                routed = dot(pick_main[j], ret[g, :, start : start + pw])
+                routed = routed + dot(pick_rem[j][f], ret[g, :, gw:])
+                acc = acc + by_position[:, 2 + j : 3 + j] * routed
+            out[:, cols] = acc.astype(BF16)
+    for arrive_b, sent_b in returns:
+        sent_b()
 
 
 def fused(geo, *args):
@@ -648,8 +697,6 @@
     rem_n = cap - TILE
     fw = width * rem_n // TILE
     rp = width // nb
-    frequencies = 10000.0 ** (-jnp.arange(hd // 2, dtype=F32) / (hd // 2))
-    inverse = jnp.concatenate([frequencies, frequencies])[None]
     vmem = pl.BlockSpec(memory_space=pltpu.VMEM)
     hbm = pl.BlockSpec(memory_space=pl.ANY)
     n_chunks = 8
@@ -657,9 +704,18 @@
     out = pl.pallas_call(
         functools.partial(fused_kernel, geo),
         out_shape=jax.ShapeDtypeStruct((rows, width), BF16),
-        in_specs=[vmem] * 10 + [hbm] * 3,
+        in_specs=[hbm] * 12,
         out_specs=vmem,
         scratch_shapes=[
+            pltpu.VMEM((rows, width), BF16),
+            pltpu.VMEM((rows, width), BF16),
+            pltpu.VMEM((rows, width), BF16),
+            pltpu.VMEM((rows, width), BF16),
+            pltpu.VMEM((heads, rows), F32),
+            pltpu.VMEM((1, width), F32),
+            pltpu.VMEM((1, width), F32),
+            pltpu.VMEM((2, rows), jnp.int32),
+            pltpu.VMEM((2, rows), F32),
             pltpu.VMEM((width, ff), BF16),
             pltpu.VMEM((width, ff), BF16),
             pltpu.VMEM((width, ff), BF16),
@@ -669,41 +725,38 @@
             pltpu.VMEM((nb, heads, hd), F32),
             pltpu.VMEM((width, hd), BF16),
             pltpu.VMEM((width, hd), BF16),
-            pltpu.VMEM((nb * TILE, width), BF16),
-            pltpu.VMEM((nb * TILE, fw), BF16),
+            pltpu.VMEM((nb * TILE, width + fw), BF16),
+            pltpu.VMEM((nb * TILE, width + fw), BF16),
             pltpu.VMEM((nb * cap, width), BF16),
-            pltpu.VMEM((nb * TILE, fw), BF16),
             pltpu.VMEM((nb * cap, ff), BF16),
-            pltpu.VMEM((nb * TILE, width), BF16),
-            pltpu.VMEM((nb * rem_n, width), BF16),
-            pltpu.VMEM((nb * TILE, fw), BF16),
-            pltpu.VMEM((nb * TILE, width), BF16),
-            pltpu.VMEM((nb * TILE, fw), BF16),
+            pltpu.VMEM((nb * rem_n, width // 2), BF16),
+            pltpu.VMEM((2, nb * TILE, (width + fw) // 2), BF16),
+            pltpu.VMEM((2, nb * TILE, (width + fw) // 2), BF16),
             pltpu.VMEM((rows, width), BF16),
             pltpu.VMEM((rows, width), BF16),
             pltpu.VMEM((rows, width), F32),
+            dma((9,)),
             dma((n_chunks,)),
             dma((n_chunks,)),
             dma((n_chunks,)),
             dma((n_chunks,)),
             dma((n_chunks,)),
-            dma((7, nb)),
-            dma((7, nb)),
+            dma((6, nb)),
+            dma((6, nb)),
         ],
         compiler_params=pltpu.CompilerParams(
-            collective_id=0, has_side_effects=True, vmem_limit_bytes=48 * 1024 * 1024
+            collective_id=0, has_side_effects=True, vmem_limit_bytes=63 * 1024 * 1024
         ),
     )(
         hidden_in[0],
         queries[0],
         keys[0],
         values[0],
-        log_decay[0],
+        log_decay[0].T,
         retention_gain[None],
         norm_gain[None],
-        inverse,
-        routes[0],
-        route_weights[0],
+        routes[0].T,
+        route_weights[0].T,
         w_gate[0],
         w_up[0],
         w_down[0],
@@ -728,7 +781,8 @@
         and experts <= 128
         and 0 < rem_n < TILE
         and TILE % rem_n == 0
-        and (width * rem_n) % (TILE * 128) == 0
+        and (width * rem_n) % (TILE * 256) == 0
+        and rem_n * 2 <= TILE
         and nb * rem_n % TILE == 0
         and hd == 128
         and rows == 128

time: 120 us -> 84.6 us (0.70)
  Pallas kernels: 106 us -> 82.1 us
  local copies, waits for them, and re-layouts: 12.3 us -> 1.67 us
    pallas_call x1, Pallas kernels: 106 us -> 82.1 us  [fused(): pl.pallas_call(functools.partial(fused_kernel, geo), out_shape=jax.ShapeD...]
    unnamed x22 -> x1, local copies, waits for them, and re-layouts: 12.3 us -> 1.67 us
where the time goes in v3:
time: 84.6 us; the launch traced here: 83.7 us
  Pallas kernels  82.1 us (97%)
  local copies, waits for them, and re-layouts  1.67 us (2%)
    pallas_call x1, Pallas kernels, fused(): pl.pallas_call(functools.partial(fused_kernel, geo), out_shape=jax.ShapeD...  82.1 us

profile of v3, /device:TPU:0, one launch (start us, length us, event | category | flops | bytes accessed | tf_op | source)
XLA Modules:
  0.0 83.7 jit_solution(11624367518255381967)
XLA Ops:
  0.0 82.1 %shard_map.118 = bf16[128,1024]{1,0:T(8,128)(2,1)} custom-call(bf16[128,1024]{1,0:T(8,128)(2,1)} %bitcast.23, bf16[128,1024]{1,0:T(8,128)(2,1)} %bitcast.24, bf16[128,1024]{1,0:T(8,128)(2,1)} %bitcast.25, bf16[128,1024]{1,0:T(8,128)(2,1)} %bitcast.26, f32[8,128]{1,0:T(8,128)} %bitcast.27, f32[1,1024]{1,0:T(1,128)} %bitcast.28, f32[1,1024]{1,0:T(1,128)} %bitcast.29, ...), custom_call_target="tpu_custom_call" | custom-call | tf_op jit(solution)/shard_map/pallas_call | solution.py:704
  82.1 1.7 %copy.14 = bf16[1,128,1024]{2,1,0:T(8,128)(2,1)} copy(bf16[1,128,1024]{2,1,0:T(8,128)(2,1)} %bitcast.22) | data formatting | bytes 524288

commit v4 on v3

--- a/solution.py
+++ b/solution.py
@@ -398,7 +398,7 @@
                 sib_copy(i, True).start()
                 local_copy(i).start()
 
-    begin(0, 1)
+    begin(0, 2)
 
     def chosen(array, group):
         found = [i for i in range(len(chunks)) if chunks[i][4] == array]
@@ -460,7 +460,7 @@
             lax.fori_loop(1, nb, one, 0)
 
         own = pl.ds(pl.multiple_of(me * n, n), n)
-        return start, arrive, sent, own
+        return start, arrive, sent, own, copy
 
     causal = iota((rows, rows), 0) >= iota((rows, rows), 1)
     upper = (iota((rows, rows), 0) <= iota((rows, rows), 1)).astype(F32)
@@ -470,6 +470,32 @@
     total = total_t.T
     last_t = total_t[:, rows - 1 : rows]
     dec_send[...] = jnp.broadcast_to(jnp.exp(last_t), dec_send.shape)
+    _, arrive_s, sent_s, own_s, slice_copy = exchange(0, sum_send, sum_recv, rp)
+
+    def dec_copy(d, landing):
+        dest = lax.rem(me + d, nb)
+        return pltpu.make_async_remote_copy(
+            src_ref=dec_send,
+            dst_ref=dec_recv.at[landing],
+            send_sem=x_send.at[1, d],
+            recv_sem=x_recv.at[1, d],
+            device_id=peer(dest),
+            device_id_type=MESH,
+        )
+
+    def dec_start(d, carry):
+        dec_copy(d, me).start()
+        return carry
+
+    def dec_arrive(d, carry):
+        dec_copy(d, lax.rem(me + nb - d, nb)).wait_recv()
+        return carry
+
+    def dec_sent(d, carry):
+        dec_copy(d, me).wait_send()
+        return carry
+
+    lax.fori_loop(1, nb, dec_start, 0)
     for h in range(heads):
         cols = slice(h * hd, (h + 1) * hd)
         q_h = q[:, cols].astype(F32)
@@ -485,35 +511,14 @@
         fine = (scaled - coarse.astype(F32)).astype(BF16)
         v_h = v[:, cols]
         sum_send[cols, :] = (dot(coarse, v_h) + dot(fine, v_h)).astype(BF16)
-
-    start_s, arrive_s, sent_s, own_s = exchange(0, sum_send, sum_recv, rp)
-
-    def dec_copy(d, landing):
-        dest = lax.rem(me + d, nb)
-        return pltpu.make_async_remote_copy(
-            src_ref=dec_send,
-            dst_ref=dec_recv.at[landing],
-            send_sem=x_send.at[1, d],
-            recv_sem=x_recv.at[1, d],
-            device_id=peer(dest),
-            device_id_type=MESH,
-        )
-
-    def dec_start(d, carry):
-        dec_copy(d, me).start()
-        return carry
-
-    def dec_arrive(d, carry):
-        dec_copy(d, lax.rem(me + nb - d, nb)).wait_recv()
-        return carry
-
-    def dec_sent(d, carry):
-        dec_copy(d, me).wait_send()
-        return carry
-
-    lax.fori_loop(1, nb, dec_start, 0)
-    start_s()
-    begin(1, 2)
+        for dest in range(h * hd // rp, (h + 1) * hd // rp):
+
+            @pl.when(me != dest)
+            def _():
+                slice_copy(lax.rem(dest + nb - me, nb), me).start()
+
+
+    begin(2, 4)
     sum_recv[own_s, :] = sum_send[own_s, :]
     dec_recv[me] = dec_send[...]
 
@@ -533,9 +538,8 @@
         ent_send[part, :] = state.astype(BF16)
         if b < nb - 1:
             state = dec_recv[b, pl.ds(head, 1), :] * state + sum_recv[part, :].astype(F32)
-    start_e, arrive_e, sent_e, own_e = exchange(2, ent_send, ent_recv, rp)
+    start_e, arrive_e, sent_e, own_e, _ = exchange(2, ent_send, ent_recv, rp)
     start_e()
-    begin(2, 4)
     for argument in arguments[4:]:
         argument.wait()
     ent_recv[own_e, :] = ent_send[own_e, :]
@@ -582,7 +586,7 @@
     for f in range(fold):
         folded = folded + dot(put_rem[f], normed[:, f * fw : (f + 1) * fw])
     disp[:, width:] = folded.astype(BF16)
-    start_m, arrive_m, sent_m, own_m = exchange(3, disp, xin, TILE)
+    start_m, arrive_m, sent_m, own_m, _ = exchange(3, disp, xin, TILE)
     start_m()
     begin(4, 8)
     xin[own_m, :] = disp[own_m, :]
@@ -635,7 +639,7 @@
             refold = (iota((nb * TILE, nb * rem_n), 0) == spot + f * rem_n).astype(F32)
             folded = folded + dot(refold.astype(BF16), orem[:, f * pw : (f + 1) * pw])
         eo[g, :, gw:] = folded.astype(BF16)
-        start_b, arrive_b, sent_b, own_b = exchange(4 + g, eo.at[g], ret.at[g], TILE)
+        start_b, arrive_b, sent_b, own_b, _ = exchange(4 + g, eo.at[g], ret.at[g], TILE)
         start_b()
         ret[g, own_b, :] = eo[g, own_b, :]
         returns.append((arrive_b, sent_b))

time: 84.6 us -> 84.9 us (level)
  the two profiles are of different devices: /device:TPU:0 before, /device:TPU:25 now
where the time goes in v4:
time: 84.9 us; the launch traced here: 84.7 us
  Pallas kernels  83 us (98%)
  local copies, waits for them, and re-layouts  1.67 us (2%)
    pallas_call x1, Pallas kernels, fused(): pl.pallas_call(functools.partial(fused_kernel, geo), out_shape=jax.ShapeD...  83 us

profile of v4, /device:TPU:25, one launch (start us, length us, event | category | flops | bytes accessed | tf_op | source)
XLA Modules:
  0.0 84.7 jit_solution(17590900378846832873)
XLA Ops:
  0.0 83.0 %shard_map.118 = bf16[128,1024]{1,0:T(8,128)(2,1)} custom-call(bf16[128,1024]{1,0:T(8,128)(2,1)} %bitcast.23, bf16[128,1024]{1,0:T(8,128)(2,1)} %bitcast.24, bf16[128,1024]{1,0:T(8,128)(2,1)} %bitcast.25, bf16[128,1024]{1,0:T(8,128)(2,1)} %bitcast.26, f32[8,128]{1,0:T(8,128)} %bitcast.27, f32[1,1024]{1,0:T(1,128)} %bitcast.28, f32[1,1024]{1,0:T(1,128)} %bitcast.29, ...), custom_call_target="tpu_custom_call" | custom-call | tf_op jit(solution)/shard_map/pallas_call | solution.py:708
  83.0 1.7 %copy.14 = bf16[1,128,1024]{2,1,0:T(8,128)(2,1)} copy(bf16[1,128,1024]{2,1,0:T(8,128)(2,1)} %bitcast.22) | data formatting | bytes 524288

commit v5 on v4

--- a/solution.py
+++ b/solution.py
@@ -614,35 +614,98 @@
         return carry
 
     lax.fori_loop(0, ff // 128, gate_up, 0)
-    groups = 2
-    part_w = half // groups
-    gw = 2 * part_w
-    pw = fw // groups
+    part_w = half // 2
+    hw = half + fw // 2
+    pw = fw // 2
     column = iota((nb * TILE, nb * rem_n), 1)
     spot = (column // rem_n) * TILE + lax.rem(column, rem_n)
-    returns = []
-    for g in range(groups):
-        hand_on(2, g)
-        take(2, g)
-
-        def down(i, carry):
-            src = pl.ds(pl.multiple_of(i * half + g * part_w, part_w), part_w)
-            cols = pl.ds(pl.multiple_of(i * part_w, part_w), part_w)
-            result = dot(hidden[...], wdb[src, :], ((1,), (1,))).astype(BF16)
-            eo[g, :, cols] = result[: nb * TILE]
-            orem[:, cols] = result[nb * TILE :]
-            return carry
-
-        lax.fori_loop(0, 2, down, 0)
+
+    def down(which, part):
+        src = pl.ds(pl.multiple_of(which * half + part * part_w, part_w), part_w)
+        cols = pl.ds(pl.multiple_of(which * hw + part * part_w, 128), part_w)
+        result = dot(hidden[...], wdb[src, :], ((1,), (1,))).astype(BF16)
+        eo[:, cols] = result[: nb * TILE]
+        orem[:, part * part_w : (part + 1) * part_w] = result[nb * TILE :]
+
+    def fold_rest(which):
         folded = jnp.zeros((nb * TILE, pw), F32)
         for f in range(fold):
             refold = (iota((nb * TILE, nb * rem_n), 0) == spot + f * rem_n).astype(F32)
             folded = folded + dot(refold.astype(BF16), orem[:, f * pw : (f + 1) * pw])
-        eo[g, :, gw:] = folded.astype(BF16)
-        start_b, arrive_b, sent_b, own_b, _ = exchange(4 + g, eo.at[g], ret.at[g], TILE)
-        start_b()
-        ret[g, own_b, :] = eo[g, own_b, :]
-        returns.append((arrive_b, sent_b))
+        eo[:, pl.ds(pl.multiple_of(which * hw + half, 128), pw)] = folded.astype(BF16)
+
+    def give_back(kind, swapped, first, span):
+        def at(ref, index, owner):
+            which = 1 - owner if swapped else owner
+            cols = pl.ds(pl.multiple_of(which * hw + first, 128), span)
+            return ref.at[pl.ds(pl.multiple_of(index * TILE, TILE), TILE), cols]
+
+        def copy(d, landing, owner):
+            dest = lax.rem(me + d, nb)
+            return pltpu.make_async_remote_copy(
+                src_ref=at(eo, dest, x),
+                dst_ref=at(ret, landing, owner),
+                send_sem=x_send.at[kind, d],
+                recv_sem=x_recv.at[kind, d],
+                device_id=peer(dest),
+                device_id_type=MESH,
+            )
+
+        def one(d, carry):
+            copy(d, me, x).start()
+            return carry
+
+        lax.fori_loop(1, nb, one, 0)
+
+        def arrive():
+            def one(d, carry):
+                source = lax.rem(me + nb - d, nb)
+                copy(d, source, lax.rem(source, exp_n)).wait_recv()
+                return carry
+
+            lax.fori_loop(1, nb, one, 0)
+
+        def sent():
+            def one(d, carry):
+                copy(d, me, x).wait_send()
+                return carry
+
+            lax.fori_loop(1, nb, one, 0)
+
+        return arrive, sent
+
+    returns = []
+
+    @pl.when(stays)
+    def _():
+        for i in chosen(2, None):
+            local_copy(i).wait()
+
+    @pl.when(moves)
+    def _():
+        for i in chosen(2, None):
+            sib_arrival(i).wait_recv()
+
+    down(x, 0)
+    down(x, 1)
+    fold_rest(x)
+    returns.append(give_back(4, False, 0, hw))
+    for part in range(2):
+        hand_on(2, part)
+
+        @pl.when(stays)
+        def _():
+            for i in chosen(2, part):
+                sib_arrival(i).wait_recv()
+
+        down(1 - x, part)
+        if part == 1:
+            fold_rest(1 - x)
+            returns.append(give_back(6, True, part_w, hw - part_w))
+        else:
+            returns.append(give_back(5, True, 0, part_w))
+    own = pl.ds(pl.multiple_of(me * TILE, TILE), TILE)
+    ret[own, :] = eo[own, :]
 
     @pl.when(moves)
     def _():
@@ -660,17 +723,16 @@
     sent_e()
     sent_m()
 
-    for g in range(groups):
-        arrive_b, sent_b = returns[g]
+    for arrive_b, sent_b in returns:
         arrive_b()
+    for which in range(2):
         for f in range(fold):
-            start = f * pw
-            into = (start // part_w) * half + g * part_w + start % part_w
-            cols = slice(into, into + pw)
+            cols = slice(which * half + f * pw, which * half + (f + 1) * pw)
+            got = slice(which * hw + f * pw, which * hw + (f + 1) * pw)
+            rest = slice(which * hw + half, (which + 1) * hw)
             acc = resid[:, cols]
             for j in range(2):
-                routed = dot(pick_main[j], ret[g, :, start : start + pw])
-                routed = routed + dot(pick_rem[j][f], ret[g, :, gw:])
+                routed = dot(pick_main[j], ret[:, got]) + dot(pick_rem[j][f], ret[:, rest])
                 acc = acc + by_position[:, 2 + j : 3 + j] * routed
             out[:, cols] = acc.astype(BF16)
     for arrive_b, sent_b in returns:
@@ -734,8 +796,8 @@
             pltpu.VMEM((nb * cap, width), BF16),
             pltpu.VMEM((nb * cap, ff), BF16),
             pltpu.VMEM((nb * rem_n, width // 2), BF16),
-            pltpu.VMEM((2, nb * TILE, (width + fw) // 2), BF16),
-            pltpu.VMEM((2, nb * TILE, (width + fw) // 2), BF16),
+            pltpu.VMEM((nb * TILE, width + fw), BF16),
+            pltpu.VMEM((nb * TILE, width + fw), BF16),
             pltpu.VMEM((rows, width), BF16),
             pltpu.VMEM((rows, width), BF16),
             pltpu.VMEM((rows, width), F32),
@@ -745,8 +807,8 @@
             dma((n_chunks,)),
             dma((n_chunks,)),
             dma((n_chunks,)),
-            dma((6, nb)),
-            dma((6, nb)),
+            dma((7, nb)),
+            dma((7, nb)),
         ],
         compiler_params=pltpu.CompilerParams(
             collective_id=0, has_side_effects=True, vmem_limit_bytes=63 * 1024 * 1024

time: 84.9 us -> 84.3 us (level)
  the two profiles are of different devices: /device:TPU:25 before, /device:TPU:0 now
where the time goes in v5:
time: 84.3 us; the launch traced here: 84.2 us
  Pallas kernels  82.5 us (98%)
  local copies, waits for them, and re-layouts  1.67 us (2%)
    pallas_call x1, Pallas kernels, fused(): pl.pallas_call(functools.partial(fused_kernel, geo), out_shape=jax.ShapeD...  82.5 us

profile of v5, /device:TPU:0, one launch (start us, length us, event | category | flops | bytes accessed | tf_op | source)
XLA Modules:
  0.0 84.2 jit_solution(2686540344991656561)
XLA Ops:
  0.0 82.5 %shard_map.118 = bf16[128,1024]{1,0:T(8,128)(2,1)} custom-call(bf16[128,1024]{1,0:T(8,128)(2,1)} %bitcast.23, bf16[128,1024]{1,0:T(8,128)(2,1)} %bitcast.24, bf16[128,1024]{1,0:T(8,128)(2,1)} %bitcast.25, bf16[128,1024]{1,0:T(8,128)(2,1)} %bitcast.26, f32[8,128]{1,0:T(8,128)} %bitcast.27, f32[1,1024]{1,0:T(1,128)} %bitcast.28, f32[1,1024]{1,0:T(1,128)} %bitcast.29, ...), custom_call_target="tpu_custom_call" | custom-call | tf_op jit(solution)/shard_map/pallas_call | solution.py:770
  82.5 1.7 %copy.14 = bf16[1,128,1024]{2,1,0:T(8,128)(2,1)} copy(bf16[1,128,1024]{2,1,0:T(8,128)(2,1)} %bitcast.22) | data formatting | bytes 524288
